TPU v7x, 512 devices: a whole 4x4x16 slice. The times are simulated.
512 devices in a mesh: row: 32 (over z, x_lo), col: 16 (over x_hi, y, core).
Axes of the slice: x: 4 (x_hi: 2, x_lo: 2; x = x_hi * 2 + x_lo), y: 4, z: 16, core: 2. Of those that a mesh axis runs over, the one named last changes fastest.
Arguments:
- vectors: float32 [64, 65536], P(None, ('row', 'col')), may hold values from -6 to 6
- blocks: bfloat16 [32, 16, 152, 128, 128], P('row', 'col'), may hold values from -0.0390625 to 0.0390625
- slot_block_rows: int32 [32, 16, 152], P('row', 'col'), may hold values from 0 to 15
- slot_block_columns: int32 [32, 16, 152], P('row', 'col'), may hold values from 0 to 31
- counts: int32 [32, 16], P('row', 'col'), may hold values from 38 to 152, as said below
Outputs:
- filtered: float32 [64, 65536], P(None, ('row', 'col'))
Inputs may be any that keep to these rules, and one draw needn't show every extreme that they name: `counts`: slots at or after a device's count carry no block.
All inputs are finite; a program needn't handle non-finite values.
Results may differ from a plain program's by a relative error of at most 0.023.
Values may be sent and summed in bfloat16 or wider, within the bound.
No kernel may reach another device: no remote copies, remote signals or barrier semaphores. Data moves between devices by JAX's collectives and lax.ppermute only.
A program may use at most 64 MiB of HBM per device.

v0:
```python
import jax
import jax.numpy as jnp
from jax import lax
from jax.sharding import PartitionSpec as P

DEGREE = 3


CENTER = 0.25
HALF_WIDTH = 2.0


def local(vectors, blocks, slot_block_rows, slot_block_columns, counts):
    width, piece_rows = vectors.shape
    block_entries = blocks[0, 0]
    rows_here = slot_block_rows[0, 0]
    cols_here = slot_block_columns[0, 0]
    live_count = counts[0, 0]
    slot_total = block_entries.shape[0]
    block_size = block_entries.shape[1]
    row_count = lax.axis_size("row")
    col_count = lax.axis_size("col")
    slab_groups = row_count // col_count
    row_index = lax.axis_index("row")
    col_index = lax.axis_index("col")
    slab_blocks = col_count * piece_rows // block_size
    col_blocks = slab_groups * slab_blocks
    slot_numbers = jnp.arange(slot_total, dtype=jnp.int32)
    global_rows = row_index * slab_blocks + rows_here
    global_cols = (
        col_index + col_count * (cols_here // slab_blocks)
    ) * slab_blocks + cols_here % slab_blocks
    live = (slot_numbers < live_count) & (global_rows <= global_cols)
    values_live = jnp.where(live[:, None, None], block_entries, jnp.zeros_like(block_entries))
    onehot_rows = (rows_here[:, None] == jnp.arange(slab_blocks, dtype=jnp.int32)[None, :]).astype(
        jnp.float32
    )
    onehot_cols = (cols_here[:, None] == jnp.arange(col_blocks, dtype=jnp.int32)[None, :]).astype(
        jnp.float32
    )

    def hamiltonian(current):
        wire = current.astype(jnp.bfloat16)
        row_slab = lax.all_gather(wire, "col", axis=1, tiled=True)
        stacked = lax.all_gather(wire, "row", axis=1, tiled=True)
        col_slab = lax.all_to_all(
            stacked.reshape(width, slab_groups, col_count, piece_rows),
            "col",
            split_axis=2,
            concat_axis=2,
            tiled=True,
        )
        col_slab = col_slab.reshape(width, col_blocks * block_size)
        inputs_col = col_slab.reshape(width, col_blocks, block_size)[:, cols_here, :]
        products = jnp.einsum(
            "sab,ksb->ksa", values_live, inputs_col, preferred_element_type=jnp.float32
        )
        row_part = jnp.einsum("sr,ksa->kra", onehot_rows, products)
        inputs_row = row_slab.reshape(width, slab_blocks, block_size)[:, rows_here, :]
        products_t = jnp.einsum(
            "sba,ksb->ksa", values_live, inputs_row, preferred_element_type=jnp.float32
        )
        col_part = jnp.einsum("sc,ksa->kca", onehot_cols, products_t)
        col_wire = col_part.astype(jnp.bfloat16).reshape(width, slab_groups, col_count, piece_rows)
        row_bf = row_part.astype(jnp.bfloat16)
        row_wire = row_bf.reshape(width, 1, col_count, piece_rows)
        row_received, received = (
            lax.all_to_all(row_wire, "col", split_axis=2, concat_axis=2, tiled=True),
            lax.all_to_all(col_wire, "col", split_axis=2, concat_axis=2, tiled=True),
        )
        row_total = jnp.sum(row_received.astype(jnp.float32), axis=(1, 2))
        flat_terms = received.reshape(width, row_count * piece_rows)
        col_total = lax.psum_scatter(flat_terms, "row", scatter_dimension=1, tiled=True).astype(
            jnp.float32
        )
        return row_total + col_total

    previous = vectors
    current = (hamiltonian(vectors) - CENTER * vectors) / HALF_WIDTH
    for degree_step in range(DEGREE - 1):
        image = hamiltonian(current)
        following = 2.0 * (image - CENTER * current) / HALF_WIDTH - previous
        previous, current = (current, following)
    return current


def solution(mesh):
    in_specs = (
        P(None, ("row", "col")),
        P("row", "col", None, None, None),
        P("row", "col", None),
        P("row", "col", None),
        P("row", "col"),
    )
    out_specs = P(None, ("row", "col"))
    return jax.shard_map(local, mesh=mesh, in_specs=in_specs, out_specs=out_specs, check_vma=False)
```

profile of v0, /device:TPU:8, one launch (start us, length us, event | category | flops | bytes accessed | tf_op | source)
XLA Modules:
  0.0 780.7 jit_solution(7533041714328886400)
XLA Ops:
  8.6 25.5 %all_gather.19 = bf16[64,2048]{1,0:T(8,128)(2,1)S(1)} all-gather(bf16[64,128]{1,0:T(8,128)(2,1)S(1)} %convert_element_type.65), channel_id=1, replica_groups=mesh['row'=32,'col'=16] {'col'}, dimensions={1}, use_global_device_ids=true | all-gather | bytes 278528 | tf_op jit(solution)/shard_map/all_gather | solution.py:44
  35.3 3.9 fusion.27
  39.2 1.6 fusion.42
  42.1 3.5 all-to-all-start.2
  45.5 73.6 %all_gather.18 = bf16[64,4096]{1,0:T(8,128)(2,1)S(1)} all-gather(bf16[64,128]{1,0:T(8,128)(2,1)S(1)} %convert_element_type.65), channel_id=1, replica_groups=mesh['row'=32,'col'=16] {'row'}, dimensions={1}, use_global_device_ids=true | all-gather | bytes 540672 | tf_op jit(solution)/shard_map/all_gather | solution.py:45
  120.3 7.0 all-to-all-start
  128.7 7.3 all-to-all-done
  137.1 5.9 fusion.24
  143.1 1.4 fusion.66
  144.6 13.4 %all_to_all.45 = bf16[64,1,16,128]{3,0,1,2:T(8,128)(2,1)S(1)} all-to-all(bf16[64,1,16,128]{3,0,1,2:T(8,128)(2,1)S(1)} %copy.44), channel_id=1, replica_groups=mesh['row'=32,'col'=16] {'col'}, dimensions={2} | all-to-all | bytes 524288 | tf_op jit(solution)/shard_map/all_to_all | solution.py:68
  158.0 104.8 %reduce-scatter.10.cloned.1.call-done = bf16[128,64]{1,0:T(8,128)(2,1)} async-done(((bf16[4096,64]{1,0:T(8,128)(2,1)}), bf16[128,64]{1,0:T(8,128)(2,1)}) %reduce-scatter.10.cloned.1.call-update) | async-done | bytes 16400
  263.7 61.7 %all_gather.20 = bf16[64,4096]{1,0:T(8,128)(2,1)S(1)} all-gather(bf16[64,128]{1,0:T(8,128)(2,1)S(1)} %multiply_convert_fusion), channel_id=1, replica_groups=mesh['row'=32,'col'=16] {'row'}, dimensions={1}, use_global_device_ids=true | all-gather | bytes 540672 | tf_op jit(solution)/shard_map/all_gather | solution.py:45
  325.4 20.4 %all_gather.21 = bf16[64,2048]{1,0:T(8,128)(2,1)S(1)} all-gather(bf16[64,128]{1,0:T(8,128)(2,1)S(1)} %multiply_convert_fusion), channel_id=1, replica_groups=mesh['row'=32,'col'=16] {'col'}, dimensions={1}, use_global_device_ids=true | all-gather | bytes 278528 | tf_op jit(solution)/shard_map/all_gather | solution.py:44
  346.9 8.2 %all-to-all-start.3 = ((bf16[64,2,16,128]{3,0,1,2:T(8,128)(2,1)}), bf16[64,2,16,128]{3,0,1,2:T(8,128)(2,1)S(1)}, u32[]{:S(2)}, u32[]{:S(2)}) async-start(bf16[64,2,16,128]{3,0,1,2:T(8,128)(2,1)} %copy.49), calls=%async_computation.3 | async-start | bytes 1048576 | tf_op jit(solution)/shard_map/all_to_all | solution.py:46
  356.2 3.9 fusion.33
  360.1 1.6 fusion.45
  364.8 7.0 all-to-all-start.5
  374.1 6.6 all-to-all-done.5
  382.1 5.9 fusion.30
  388.0 1.4 fusion.63
  389.5 13.2 %all_to_all.46 = bf16[64,1,16,128]{3,0,1,2:T(8,128)(2,1)S(1)} all-to-all(bf16[64,1,16,128]{3,0,1,2:T(8,128)(2,1)S(1)} %copy.52), channel_id=1, replica_groups=mesh['row'=32,'col'=16] {'col'}, dimensions={2} | all-to-all | bytes 524288 | tf_op jit(solution)/shard_map/all_to_all | solution.py:68
  402.8 114.9 %reduce-scatter.12.cloned.1.call-done = bf16[128,64]{1,0:T(8,128)(2,1)} async-done(((bf16[4096,64]{1,0:T(8,128)(2,1)}), bf16[128,64]{1,0:T(8,128)(2,1)}) %reduce-scatter.12.cloned.1.call-update) | async-done | bytes 16400
  518.6 61.7 %all_gather.22 = bf16[64,4096]{1,0:T(8,128)(2,1)S(1)} all-gather(bf16[64,128]{1,0:T(8,128)(2,1)S(1)} %fusion.84), channel_id=1, replica_groups=mesh['row'=32,'col'=16] {'row'}, dimensions={1}, use_global_device_ids=true | all-gather | bytes 540672 | tf_op jit(solution)/shard_map/all_gather | solution.py:45
  580.3 20.5 %all_gather.23 = bf16[64,2048]{1,0:T(8,128)(2,1)S(1)} all-gather(bf16[64,128]{1,0:T(8,128)(2,1)S(1)} %fusion.84), channel_id=1, replica_groups=mesh['row'=32,'col'=16] {'col'}, dimensions={1}, use_global_device_ids=true | all-gather | bytes 278528 | tf_op jit(solution)/shard_map/all_gather | solution.py:44
  601.9 8.1 %all-to-all-start.6 = ((bf16[64,2,16,128]{3,0,1,2:T(8,128)(2,1)}), bf16[64,2,16,128]{3,0,1,2:T(8,128)(2,1)S(1)}, u32[]{:S(2)}, u32[]{:S(2)}) async-start(bf16[64,2,16,128]{3,0,1,2:T(8,128)(2,1)} %copy.57), calls=%async_computation.6 | async-start | bytes 1048576 | tf_op jit(solution)/shard_map/all_to_all | solution.py:46
  611.3 3.9 fusion.39
  615.2 1.6 fusion.48
  619.7 7.0 all-to-all-start.8
  629.1 6.6 all-to-all-done.8
  637.0 5.9 fusion.36
  644.5 13.2 %all_to_all.47 = bf16[64,1,16,128]{3,0,1,2:T(8,128)(2,1)S(1)} all-to-all(bf16[64,1,16,128]{3,0,1,2:T(8,128)(2,1)S(1)} %copy.60), channel_id=1, replica_groups=mesh['row'=32,'col'=16] {'col'}, dimensions={2} | all-to-all | bytes 524288 | tf_op jit(solution)/shard_map/all_to_all | solution.py:68
  657.7 114.9 %reduce-scatter.14.cloned.1.call-done = bf16[128,64]{1,0:T(8,128)(2,1)} async-done(((bf16[4096,64]{1,0:T(8,128)(2,1)}), bf16[128,64]{1,0:T(8,128)(2,1)}) %reduce-scatter.14.cloned.1.call-update) | async-done | bytes 16400
  (96 shorter events, 30.3 us)
Async XLA Ops:
  8.6 346.5 %copy-start.12 = (s32[1024]{0:T(1024)}, s32[1024]{0:T(1024)S(1)}, u32[]{:S(2)}) copy-start(s32[1024]{0:T(1024)S(1)} %pad_clamp_fusion) | copy-start | bytes 12292
  34.2 1.1 copy-start.14
  34.2 1.1 copy-start.16
  35.3 320.9 %copy-start.19 = (pred[152]{0:T(512)(128)(4,1)}, pred[152]{0:T(512)(128)(4,1)S(1)}, u32[]{:S(2)}) copy-start(pred[152]{0:T(512)(128)(4,1)S(1)} %compare_and_fusion) | copy-start | bytes 460
  42.1 78.2 %all-to-all-start.2 = ((bf16[64,2,16,128]{3,1,0,2:T(2,128)(2,1)}), bf16[64,2,16,128]{3,1,0,2:T(2,128)(2,1)S(1)}, u32[]{:S(2)}, u32[]{:S(2)}) async-start(bf16[64,2,16,128]{3,1,0,2:T(2,128)(2,1)} %copy.47), calls=%async_computation.2 | async-start | bytes 1048576 | tf_op jit(solution)/shard_map/all_to_all | solution.py:69
  120.3 15.8 %all-to-all-start = ((bf16[64,2,16,128]{3,0,1,2:T(8,128)(2,1)}), bf16[64,2,16,128]{3,0,1,2:T(8,128)(2,1)S(1)}, u32[]{:S(2)}, u32[]{:S(2)}) async-start(bf16[64,2,16,128]{3,0,1,2:T(8,128)(2,1)} %copy.41), calls=%async_computation | async-start | bytes 1048576 | tf_op jit(solution)/shard_map/all_to_all | solution.py:46
  127.2 135.5 %reduce-scatter.10.cloned.1.call-start = ((), (), s32[]{:S(2)}) async-start(), calls=%async_computation.12 | async-start | bytes 1081344
  127.3 15.7 %copy-start.13 = (s32[1024]{0:T(1024)}, s32[1024]{0:T(1024)S(1)}, u32[]{:S(2)}) copy-start(s32[1024]{0:T(1024)S(1)} %pad_clamp_fusion.1) | copy-start | bytes 12292
  143.0 120.6 %copy-start.2 = (f32[64,128]{1,0:T(8,128)S(1)}, f32[64,128]{1,0:T(8,128)}, u32[]{:S(2)}) copy-start(f32[64,128]{1,0:T(8,128)} %param.5) | copy-start | bytes 98308
  158.0 105.7 %copy-start.5 = (f32[64,128]{1,0:T(8,128)}, f32[64,128]{1,0:T(8,128)S(1)}, u32[]{:S(2)}) copy-start(f32[64,128]{1,0:T(8,128)S(1)} %convert_reduce_fusion.2) | copy-start | bytes 98308
  346.9 17.1 %all-to-all-start.3 = ((bf16[64,2,16,128]{3,0,1,2:T(8,128)(2,1)}), bf16[64,2,16,128]{3,0,1,2:T(8,128)(2,1)S(1)}, u32[]{:S(2)}, u32[]{:S(2)}) async-start(bf16[64,2,16,128]{3,0,1,2:T(8,128)(2,1)} %copy.49), calls=%async_computation.3 | async-start | bytes 1048576 | tf_op jit(solution)/shard_map/all_to_all | solution.py:46
  364.0 0.8 copy-start.1
  364.8 15.9 %all-to-all-start.5 = ((bf16[64,2,16,128]{3,1,0,2:T(2,128)(2,1)}), bf16[64,2,16,128]{3,1,0,2:T(2,128)(2,1)S(1)}, u32[]{:S(2)}, u32[]{:S(2)}) async-start(bf16[64,2,16,128]{3,1,0,2:T(2,128)(2,1)} %copy.55), calls=%async_computation.5 | async-start | bytes 1048576 | tf_op jit(solution)/shard_map/all_to_all | solution.py:69
  371.8 145.9 %reduce-scatter.12.cloned.1.call-start = ((), (), s32[]{:S(2)}) async-start(), calls=%async_computation.13 | async-start | bytes 1081344
  374.1 7.9 %copy-start.20 = (pred[152]{0:T(512)(128)(4,1)S(1)}, pred[152]{0:T(512)(128)(4,1)}, u32[]{:S(2)}) copy-start(pred[152]{0:T(512)(128)(4,1)} %copy-done.19) | copy-start | bytes 460
  382.1 5.9 copy-start.17
  388.0 130.5 %copy-start.3 = (f32[64,128]{1,0:T(8,128)S(1)}, f32[64,128]{1,0:T(8,128)}, u32[]{:S(2)}) copy-start(f32[64,128]{1,0:T(8,128)} %param.5) | copy-start | bytes 98308
  388.0 130.5 %copy-start.6 = (f32[64,128]{1,0:T(8,128)S(1)}, f32[64,128]{1,0:T(8,128)}, u32[]{:S(2)}) copy-start(f32[64,128]{1,0:T(8,128)} %copy-done.5) | copy-start | bytes 98308
  402.8 199.2 %copy-start.8 = (f32[64,128]{1,0:T(8,128)}, f32[64,128]{1,0:T(8,128)S(1)}, u32[]{:S(2)}) copy-start(f32[64,128]{1,0:T(8,128)S(1)} %convert_reduce_fusion.1) | copy-start | bytes 98308
  518.6 83.4 %copy-start.10 = (bf16[64,128]{1,0:T(8,128)(2,1)}, bf16[64,128]{1,0:T(8,128)(2,1)S(1)}, u32[]{:S(2)}) copy-start(bf16[64,128]{1,0:T(8,128)(2,1)S(1)} %copy.68) | copy-start | bytes 49156
  601.9 17.0 %all-to-all-start.6 = ((bf16[64,2,16,128]{3,0,1,2:T(8,128)(2,1)}), bf16[64,2,16,128]{3,0,1,2:T(8,128)(2,1)S(1)}, u32[]{:S(2)}, u32[]{:S(2)}) async-start(bf16[64,2,16,128]{3,0,1,2:T(8,128)(2,1)} %copy.57), calls=%async_computation.6 | async-start | bytes 1048576 | tf_op jit(solution)/shard_map/all_to_all | solution.py:46
  611.3 3.9 copy-start.15
  618.9 0.8 copy-start
  619.7 15.9 %all-to-all-start.8 = ((bf16[64,2,16,128]{3,1,0,2:T(2,128)(2,1)}), bf16[64,2,16,128]{3,1,0,2:T(2,128)(2,1)S(1)}, u32[]{:S(2)}, u32[]{:S(2)}) async-start(bf16[64,2,16,128]{3,1,0,2:T(2,128)(2,1)} %copy.63), calls=%async_computation.8 | async-start | bytes 1048576 | tf_op jit(solution)/shard_map/all_to_all | solution.py:69
  626.7 145.9 %reduce-scatter.14.cloned.1.call-start = ((), (), s32[]{:S(2)}) async-start(), calls=%async_computation.14 | async-start | bytes 1081344
  629.0 7.9 %copy-start.21 = (pred[152]{0:T(512)(128)(4,1)S(1)}, pred[152]{0:T(512)(128)(4,1)}, u32[]{:S(2)}) copy-start(pred[152]{0:T(512)(128)(4,1)} %copy-done.19) | copy-start | bytes 460
  637.0 5.9 copy-start.18
  642.9 130.5 %copy-start.4 = (f32[64,128]{1,0:T(8,128)S(1)}, f32[64,128]{1,0:T(8,128)}, u32[]{:S(2)}) copy-start(f32[64,128]{1,0:T(8,128)} %param.5) | copy-start | bytes 98308
  642.9 130.5 %copy-start.7 = (f32[64,128]{1,0:T(8,128)S(1)}, f32[64,128]{1,0:T(8,128)}, u32[]{:S(2)}) copy-start(f32[64,128]{1,0:T(8,128)} %copy-done.5) | copy-start | bytes 98308
  642.9 130.5 %copy-start.9 = (f32[64,128]{1,0:T(8,128)S(1)}, f32[64,128]{1,0:T(8,128)}, u32[]{:S(2)}) copy-start(f32[64,128]{1,0:T(8,128)} %copy-done.8) | copy-start | bytes 98308
  643.0 130.5 %copy-start.11 = (bf16[64,128]{1,0:T(8,128)(2,1)S(1)}, bf16[64,128]{1,0:T(8,128)(2,1)}, u32[]{:S(2)}) copy-start(bf16[64,128]{1,0:T(8,128)(2,1)} %copy-done.10) | copy-start | bytes 49156
Sparse Core Ops, SparseCore 0:
  130.9 131.8 reduce-scatter.9
  382.2 135.4 reduce-scatter.11
  637.1 135.4 reduce-scatter.13
where the time goes:
time: 782 us; the launch traced here: 781 us
  waiting for transfers between devices  357 us (46%)
  blocking collectives  303 us (39%)
  starting transfers between devices  40.9 us (5%)
  matrix products  38.4 us (5%)
  local copies, waits for them, and re-layouts  24.6 us (3%)
  between operations  14.3 us (2%)
    unnamed x6, waiting for transfers between devices  335 us
    all_gather x3, blocking collectives, hamiltonian(): stacked = lax.all_gather(wire, 'row', axis=1, tiled=True)  197 us
    all_gather x3, blocking collectives, hamiltonian(): row_slab = lax.all_gather(wire, 'col', axis=1, tiled=True)  66.4 us
    all_to_all x3, blocking collectives, hamiltonian(): lax.all_to_all(row_wire, 'col', split_axis=2, concat_axis=2, tiled=True)  39.8 us
    all_to_all x3, starting transfers between devices, hamiltonian(): lax.all_to_all(stacked.reshape(width, slab_groups, col_count, piece_rows)...  23.3 us
    dot_general x3, matrix products, hamiltonian(): jnp.einsum('sab,ksb->ksa', values_live, inputs_col, preferred_element_typ...  17.7 us
    all_to_all x3, starting transfers between devices, hamiltonian(): lax.all_to_all(col_wire, 'col', split_axis=2, concat_axis=2, tiled=True)  17.5 us
  transfers between devices with their start and end apart: 9, of which 8 were waited for; matrix products, arithmetic and copies ran while one was open for 6% of the time, Pallas kernels for 0%

commit v1 on v0

v1 whole, which is shorter than its diff:
```python
import jax
import jax.numpy as jnp
from jax import lax
from jax.experimental import pallas as pl
from jax.experimental.pallas import tpu as pltpu
from jax.sharding import Mesh, PartitionSpec as P

CENTER = 0.25
HALF_WIDTH = 2.0
DEGREE = 3
UNROLL = 4
ROW = ("zh", "zl", "xl")
COL = ("xh", "y", "core")
FAR = "zh"
NEAR = ("zl", "xl")
ALL = ROW + COL


def term_kernel(transposed, sources, targets, x_ref, blocks_ref, out_ref, acc):
    acc[...] = jnp.zeros_like(acc)
    contract = (((1,), (1,)), ((), ())) if transposed else (((1,), (0,)), ((), ()))

    def body(step, carry):
        products = []
        for u in range(UNROLL):
            s = step * UNROLL + u
            products.append(
                lax.dot_general(x_ref[sources[s]], blocks_ref[s], contract, preferred_element_type=jnp.float32)
            )
        for u in range(UNROLL):
            t = targets[step * UNROLL + u]
            acc[t] = acc[t] + products[u]
        return carry

    lax.fori_loop(0, blocks_ref.shape[0] // UNROLL, body, 0)
    out_ref[...] = acc[: out_ref.shape[0]].astype(out_ref.dtype)


def terms(x, blocks, sources, targets, count, transposed):
    slots, size = blocks.shape[:2]
    width = x.shape[1]
    smem = pl.BlockSpec(memory_space=pltpu.SMEM)
    vmem = pl.BlockSpec(memory_space=pltpu.VMEM)
    return pl.pallas_call(
        lambda *refs: term_kernel(transposed, *refs),
        out_shape=jax.ShapeDtypeStruct((count, width, size), jnp.bfloat16),
        in_specs=[smem, smem, vmem, vmem],
        out_specs=vmem,
        scratch_shapes=[pltpu.VMEM((count + 1, width, size), jnp.float32)],
        compiler_params=pltpu.CompilerParams(vmem_limit_bytes=32 * 1024 * 1024),
        cost_estimate=pl.CostEstimate(
            flops=2 * slots * width * size * size, bytes_accessed=2 * slots * size * size, transcendentals=0
        ),
        name="row_terms" if transposed else "col_terms",
    )(sources, targets, x, blocks)


def spread(x, axes, n):
    copies = jnp.broadcast_to(x[None], (n,) + x.shape)
    return lax.all_to_all(copies, axes, 0, 0, tiled=True)


def collect(parts, axes):
    received = lax.all_to_all(parts, axes, 0, 0, tiled=True)
    return jnp.sum(received.astype(jnp.float32), axis=0)


def local(vectors, blocks, slot_block_rows, slot_block_columns, counts):
    width, size = vectors.shape
    blocks = blocks[0, 0]
    rows_here = slot_block_rows[0, 0]
    cols_here = slot_block_columns[0, 0]
    slots = blocks.shape[0]
    n_row, n_col = lax.axis_size(ROW), lax.axis_size(COL)
    n_far, n_near = lax.axis_size(FAR), lax.axis_size(NEAR)
    row, col = lax.axis_index(ROW), lax.axis_index(COL)
    global_rows = row * n_col + rows_here
    global_cols = (col + n_col * (cols_here // n_col)) * n_col + cols_here % n_col
    live = (jnp.arange(slots, dtype=jnp.int32) < counts[0, 0]) & (global_rows <= global_cols)
    cols_at = (cols_here % n_near) * n_far + cols_here // n_near
    row_targets = jnp.where(live, rows_here, n_col)
    col_targets = jnp.where(live, cols_at, n_row)
    swap = [
        ((h * n_col + i) * n_col + j, (h * n_col + j) * n_col + i)
        for h in range(n_row // n_col)
        for i in range(n_col)
        for j in range(n_col)
    ]

    def swapped(x):
        return lax.ppermute(x.astype(jnp.bfloat16), ALL, swap)

    def column_terms(wire):
        row_slab = spread(wire, COL, n_col)
        out = terms(row_slab, blocks, rows_here, col_targets, n_row, False)
        if n_far == 1:
            return collect(out, ROW)
        out = collect(out.reshape(n_near, n_far, width, size), NEAR).astype(jnp.bfloat16)
        return collect(out, FAR)

    def row_terms(wire):
        if n_far == 1:
            col_slab = spread(wire, ROW, n_row)
        else:
            col_slab = spread(spread(wire, FAR, n_far), NEAR, n_near).reshape(n_row, width, size)
        out = terms(col_slab, blocks, cols_at, row_targets, n_col, True)
        return collect(out, COL)

    before = (None, None)
    now = (vectors, swapped(vectors).astype(jnp.float32))
    for step in range(DEGREE):
        col_total = column_terms(now[0].astype(jnp.bfloat16))
        row_total = row_terms(now[1].astype(jnp.bfloat16))
        image = [row_total + swapped(col_total).astype(jnp.float32), None]
        if step < DEGREE - 1:
            image[1] = col_total + swapped(row_total).astype(jnp.float32)
        if step == 0:
            after = [None if h is None else (h - CENTER * x) / HALF_WIDTH for h, x in zip(image, now)]
        else:
            after = [
                None if h is None else 2.0 * (h - CENTER * x) / HALF_WIDTH - b for h, x, b in zip(image, now, before)
            ]
        before, now = now, after
    return now[0]


def solution(mesh):
    split = Mesh(mesh.devices.reshape(4, 4, 2, 2, 4, 2), ALL)
    in_specs = (
        P(None, ALL),
        P(ROW, COL, None, None, None),
        P(ROW, COL, None),
        P(ROW, COL, None),
        P(ROW, COL),
    )
    return jax.shard_map(local, mesh=split, in_specs=in_specs, out_specs=P(None, ALL), check_vma=False)
```

time: 782 us -> 394 us (0.50)
  the two profiles are of different devices: /device:TPU:8 before, /device:TPU:28 now
where the time goes in v1:
time: 394 us; the launch traced here: 392 us
  starting transfers between devices  141 us (36%)
  waiting for transfers between devices  93.3 us (24%)
  blocking collectives  82.1 us (21%)
  Pallas kernels  49.8 us (13%)
  local copies, waits for them, and re-layouts  20 us (5%)
  other arithmetic  4.47 us (1%)
    ppermute x6, starting transfers between devices, swapped(): return lax.ppermute(x.astype(jnp.bfloat16), ALL, swap)  53.3 us
    all_to_all x3, blocking collectives, spread(): return lax.all_to_all(copies, axes, 0, 0, tiled=True)  51.3 us
    pallas_call x6, Pallas kernels, terms(): pl.pallas_call(lambda *refs: term_kernel(transposed, *refs), out_shape=ja...  49.8 us
    all_to_all x7, starting transfers between devices, collect(): received = lax.all_to_all(parts, axes, 0, 0, tiled=True)  48.1 us
    ppermute x6, waiting for transfers between devices, swapped(): return lax.ppermute(x.astype(jnp.bfloat16), ALL, swap)  47.2 us
    all_to_all x6, starting transfers between devices, spread(): return lax.all_to_all(copies, axes, 0, 0, tiled=True)  39.9 us
    all_to_all x6, waiting for transfers between devices, spread(): return lax.all_to_all(copies, axes, 0, 0, tiled=True)  35.3 us
    all_to_all x2, blocking collectives, collect(): received = lax.all_to_all(parts, axes, 0, 0, tiled=True)  30.8 us
  transfers between devices with their start and end apart: 19, of which 16 were waited for; matrix products, arithmetic and copies ran while one was open for 1% of the time, Pallas kernels for 13%

profile of v1, /device:TPU:28, one launch (start us, length us, event | category | flops | bytes accessed | tf_op | source)
XLA Modules:
  0.0 392.0 jit_solution(10784165700845562152)
XLA Ops:
  0.8 12.7 %collective-permute-start = (bf16[64,128]{1,0:T(8,128)(2,1)S(1)}, bf16[64,128]{1,0:T(8,128)(2,1)S(1)}, u32[]{:S(2)}, u32[]{:S(2)}) collective-permute-start(bf16[64,128]{1,0:T(8,128)(2,1)S(1)} %convert_element_type.70), channel_id=1, source_target_pairs={{0,0},{1,16},{2,32},{3,48},{4,64},{5,80},{6,96},{7,112},{8,128},{9... | collective-permute-start | bytes 49160 | tf_op jit(solution)/shard_map/ppermute | solution.py:91
  17.5 27.9 %all_to_all.90 = bf16[4,64,128]{2,1,0:T(8,128)(2,1)S(1)} all-to-all(bf16[4,64,128]{2,1,0:T(8,128)(2,1)S(1)} %broadcast_in_dim.24), channel_id=1, replica_groups=mesh['zh'=4,'zl'=4,'xl'=2,'xh'=2,'y'=4,'core'=2] {'zh'}, dimensions={0} | all-to-all | bytes 131072 | tf_op jit(solution)/shard_map/all_to_all | solution.py:60
  45.5 11.7 %all_to_all.91.refs_2_ = bf16[16,64,128]{2,1,0:T(8,128)(2,1)S(1)} all-to-all(bf16[16,64,128]{2,1,0:T(8,128)(2,1)S(1)} %broadcast_in_dim.26), channel_id=1, replica_groups=mesh['zh'=4,'zl'=4,'xl'=2,'xh'=2,'y'=4,'core'=2] {'xh','y','core'}, dimensions={0} | all-to-all | bytes 524288 | tf_op jit(solution)/shard_map/all_to_all | solution.py:60
  66.1 8.0 %col_terms.3 = bf16[32,64,128]{2,1,0:T(8,128)(2,1)} custom-call(s32[152]{0:T(256)S(1)} %bitcast.23, s32[152]{0:T(256)S(1)} %get-tuple-element.5.refs_1_, bf16[16,64,128]{2,1,0:T(8,128)(2,1)S(1)} %all_to_all.91.refs_2_, bf16[152,128,128]{2,1,0:T(8,128)(2,1)S(1)} %bitcast.11), custom_call_target="tpu_custom_call" | custom-call | flops 318767104 | bytes 4980736 | tf_op jit(solution)/shard_map/col_terms/pallas_call | solution.py:44
  82.8 9.1 %row_terms.3 = bf16[16,64,128]{2,1,0:T(8,128)(2,1)} custom-call(s32[152]{0:T(256)S(1)} %get-tuple-element.7.refs_0_, s32[152]{0:T(256)S(1)} %broadcast_select_fusion.1.refs_1_, bf16[32,64,128]{2,1,0:T(8,128)(2,1)S(1)} %bitcast.17, bf16[152,128,128]{2,1,0:T(8,128)(2,1)S(1)} %bitcast.12), custom_call_target="tpu_custom_call" | custom-call | flops 318767104 | bytes 4980736 | tf_op jit(solution)/shard_map/row_terms/pallas_call | solution.py:44
  95.1 7.3 %all-to-all-start.2 = ((bf16[16,64,128]{2,1,0:T(8,128)(2,1)}), bf16[16,64,128]{2,1,0:T(8,128)(2,1)S(1)}, u32[]{:S(2)}, u32[]{:S(2)}) async-start(bf16[16,64,128]{2,1,0:T(8,128)(2,1)} %row_terms.3), calls=%async_computation.2 | async-start | bytes 524288 | tf_op jit(solution)/shard_map/all_to_all | solution.py:64
  103.1 4.2 %all-to-all-done.2 = bf16[16,64,128]{2,1,0:T(8,128)(2,1)S(1)} async-done(((bf16[16,64,128]{2,1,0:T(8,128)(2,1)}), bf16[16,64,128]{2,1,0:T(8,128)(2,1)S(1)}, u32[]{:S(2)}, u32[]{:S(2)}) %all-to-all-start.2) | async-done | bytes 262176 | tf_op jit(solution)/shard_map/all_to_all | solution.py:64
  110.7 12.5 %collective-permute-start.2 = (bf16[64,128]{1,0:T(8,128)(2,1)S(1)}, bf16[64,128]{1,0:T(8,128)(2,1)S(1)}, u32[]{:S(2)}, u32[]{:S(2)}) collective-permute-start(bf16[64,128]{1,0:T(8,128)(2,1)S(1)} %convert_element_type.77), channel_id=1, source_target_pairs={{0,0},{1,16},{2,32},{3,48},{4,64},{5,80},{6,96},{7,112},{8,128},{9... | collective-permute-start | bytes 49160 | tf_op jit(solution)/shard_map/ppermute | solution.py:91
  123.7 4.4 %collective-permute-done.2 = bf16[64,128]{1,0:T(8,128)(2,1)S(1)} collective-permute-done((bf16[64,128]{1,0:T(8,128)(2,1)S(1)}, bf16[64,128]{1,0:T(8,128)(2,1)S(1)}, u32[]{:S(2)}, u32[]{:S(2)}) %collective-permute-start.2) | collective-permute-done | bytes 16416 | tf_op jit(solution)/shard_map/ppermute | solution.py:91
  128.1 11.9 %collective-permute-start.1 = (bf16[64,128]{1,0:T(8,128)(2,1)S(1)}, bf16[64,128]{1,0:T(8,128)(2,1)S(1)}, u32[]{:S(2)}, u32[]{:S(2)}) collective-permute-start(bf16[64,128]{1,0:T(8,128)(2,1)S(1)} %get-tuple-element.11), channel_id=1, source_target_pairs={{0,0},{1,16},{2,32},{3,48},{4,64},{5,80},{6,96},{7,112},{8,128},{9... | collective-permute-start | bytes 49160 | tf_op jit(solution)/shard_map/ppermute | solution.py:91
  140.0 4.9 %collective-permute-done.1 = bf16[64,128]{1,0:T(8,128)(2,1)S(1)} collective-permute-done((bf16[64,128]{1,0:T(8,128)(2,1)S(1)}, bf16[64,128]{1,0:T(8,128)(2,1)S(1)}, u32[]{:S(2)}, u32[]{:S(2)}) %collective-permute-start.1) | collective-permute-done | bytes 16416 | tf_op jit(solution)/shard_map/ppermute | solution.py:91
  144.9 11.7 %all_to_all.92.refs_2_ = bf16[16,64,128]{2,1,0:T(8,128)(2,1)S(1)} all-to-all(bf16[16,64,128]{2,1,0:T(8,128)(2,1)S(1)} %broadcast_in_dim.27), channel_id=1, replica_groups=mesh['zh'=4,'zl'=4,'xl'=2,'xh'=2,'y'=4,'core'=2] {'xh','y','core'}, dimensions={0} | all-to-all | bytes 524288 | tf_op jit(solution)/shard_map/all_to_all | solution.py:60
  157.3 11.4 %all-to-all-start.9 = ((bf16[4,64,128]{2,1,0:T(8,128)(2,1)}), bf16[4,64,128]{2,1,0:T(8,128)(2,1)S(1)}, u32[]{:S(2)}, u32[]{:S(2)}) async-start(bf16[4,64,128]{2,1,0:T(8,128)(2,1)} %broadcast_in_dim.28), calls=%async_computation.9 | async-start | bytes 131072 | tf_op jit(solution)/shard_map/all_to_all | solution.py:60
  171.1 7.2 %col_terms.4 = bf16[32,64,128]{2,1,0:T(8,128)(2,1)S(1)} custom-call(s32[152]{0:T(256)S(1)} %bitcast.25, s32[152]{0:T(256)S(1)} %get-tuple-element.5.refs_1_, bf16[16,64,128]{2,1,0:T(8,128)(2,1)S(1)} %all_to_all.92.refs_2_, bf16[152,128,128]{2,1,0:T(8,128)(2,1)S(1)} %bitcast.13), custom_call_target="tpu_custom_call" | custom-call | flops 318767104 | bytes 4980736 | tf_op jit(solution)/shard_map/col_terms/pallas_call | solution.py:44
  181.7 16.2 %all_to_all.93 = bf16[8,4,64,128]{3,2,1,0:T(8,128)(2,1)S(1)} all-to-all(bf16[8,4,64,128]{3,2,1,0:T(8,128)(2,1)S(1)} %bitcast.21), channel_id=1, replica_groups=mesh['zh'=4,'zl'=4,'xl'=2,'xh'=2,'y'=4,'core'=2] {'zl','xl'}, dimensions={0} | all-to-all | bytes 1048576 | tf_op jit(solution)/shard_map/all_to_all | solution.py:64
  203.2 13.4 %all-to-all-done.10 = bf16[8,4,64,128]{3,2,1,0:T(8,128)(2,1)S(1)} async-done(((bf16[8,4,64,128]{3,2,1,0:T(8,128)(2,1)}), bf16[8,4,64,128]{3,2,1,0:T(8,128)(2,1)S(1)}, u32[]{:S(2)}, u32[]{:S(2)}) %all-to-all-start.10) | async-done | bytes 524320 | tf_op jit(solution)/shard_map/all_to_all | solution.py:60
  216.5 9.6 %all-to-all-start.8 = ((bf16[4,64,128]{2,1,0:T(8,128)(2,1)}), bf16[4,64,128]{2,1,0:T(8,128)(2,1)S(1)}, u32[]{:S(2)}, u32[]{:S(2)}) async-start(bf16[4,64,128]{2,1,0:T(8,128)(2,1)} %reduce_sum.96), calls=%async_computation.8 | async-start | bytes 131072 | tf_op jit(solution)/shard_map/all_to_all | solution.py:64
  228.6 9.1 %row_terms.4 = bf16[16,64,128]{2,1,0:T(8,128)(2,1)} custom-call(s32[152]{0:T(256)S(1)} %get-tuple-element.7.refs_0_, s32[152]{0:T(256)S(1)} %broadcast_select_fusion.1.refs_1_, bf16[32,64,128]{2,1,0:T(8,128)(2,1)S(1)} %bitcast.19, bf16[152,128,128]{2,1,0:T(8,128)(2,1)S(1)} %bitcast.14), custom_call_target="tpu_custom_call" | custom-call | flops 318767104 | bytes 4980736 | tf_op jit(solution)/shard_map/row_terms/pallas_call | solution.py:44
  239.2 7.2 %all-to-all-start.11 = ((bf16[16,64,128]{2,1,0:T(8,128)(2,1)}), bf16[16,64,128]{2,1,0:T(8,128)(2,1)S(1)}, u32[]{:S(2)}, u32[]{:S(2)}) async-start(bf16[16,64,128]{2,1,0:T(8,128)(2,1)} %row_terms.4), calls=%async_computation.11 | async-start | bytes 524288 | tf_op jit(solution)/shard_map/all_to_all | solution.py:64
  246.4 6.5 %collective-permute-start.4 = (bf16[64,128]{1,0:T(8,128)(2,1)S(1)}, bf16[64,128]{1,0:T(8,128)(2,1)S(1)}, u32[]{:S(2)}, u32[]{:S(2)}) collective-permute-start(bf16[64,128]{1,0:T(8,128)(2,1)S(1)} %convert_element_type.86), channel_id=1, source_target_pairs={{0,0},{1,16},{2,32},{3,48},{4,64},{5,80},{6,96},{7,112},{8,128},{9... | collective-permute-start | bytes 49160 | tf_op jit(solution)/shard_map/ppermute | solution.py:91
  253.0 10.2 %collective-permute-done.4 = bf16[64,128]{1,0:T(8,128)(2,1)S(1)} collective-permute-done((bf16[64,128]{1,0:T(8,128)(2,1)S(1)}, bf16[64,128]{1,0:T(8,128)(2,1)S(1)}, u32[]{:S(2)}, u32[]{:S(2)}) %collective-permute-start.4) | collective-permute-done | bytes 16416 | tf_op jit(solution)/shard_map/ppermute | solution.py:91
  263.9 6.9 %all-to-all-start.15 = ((bf16[16,64,128]{2,1,0:T(8,128)(2,1)}), bf16[16,64,128]{2,1,0:T(8,128)(2,1)S(1)}, u32[]{:S(2)}, u32[]{:S(2)}) async-start(bf16[16,64,128]{2,1,0:T(8,128)(2,1)} %broadcast_in_dim.32), calls=%async_computation.15 | async-start | bytes 524288 | tf_op jit(solution)/shard_map/all_to_all | solution.py:60
  274.0 13.6 %collective-permute-done.3 = bf16[64,128]{1,0:T(8,128)(2,1)S(1)} collective-permute-done((bf16[64,128]{1,0:T(8,128)(2,1)S(1)}, bf16[64,128]{1,0:T(8,128)(2,1)S(1)}, u32[]{:S(2)}, u32[]{:S(2)}) %collective-permute-start.3) | collective-permute-done | bytes 16416 | tf_op jit(solution)/shard_map/ppermute | solution.py:91
  288.2 10.7 %all-to-all-start.12 = ((bf16[4,64,128]{2,1,0:T(8,128)(2,1)}), bf16[4,64,128]{2,1,0:T(8,128)(2,1)S(1)}, u32[]{:S(2)}, u32[]{:S(2)}) async-start(bf16[4,64,128]{2,1,0:T(8,128)(2,1)} %broadcast_in_dim.30), calls=%async_computation.12 | async-start | bytes 131072 | tf_op jit(solution)/shard_map/all_to_all | solution.py:60
  301.4 7.2 %col_terms.5 = bf16[32,64,128]{2,1,0:T(8,128)(2,1)S(1)} custom-call(s32[152]{0:T(256)S(1)} %bitcast.26, s32[152]{0:T(256)S(1)} %get-tuple-element.5.refs_1_, bf16[16,64,128]{2,1,0:T(8,128)(2,1)S(1)} %all-to-all-done.15.refs_2_, bf16[152,128,128]{2,1,0:T(8,128)(2,1)S(1)} %bitcast.15), custom_call_target="tpu_custom_call" | custom-call | flops 318767104 | bytes 4980736 | tf_op jit(solution)/shard_map/col_terms/pallas_call | solution.py:44
  312.0 14.6 %all_to_all.94 = bf16[8,4,64,128]{3,2,1,0:T(8,128)(2,1)S(1)} all-to-all(bf16[8,4,64,128]{3,2,1,0:T(8,128)(2,1)S(1)} %bitcast.20), channel_id=1, replica_groups=mesh['zh'=4,'zl'=4,'xl'=2,'xh'=2,'y'=4,'core'=2] {'zl','xl'}, dimensions={0} | all-to-all | bytes 1048576 | tf_op jit(solution)/shard_map/all_to_all | solution.py:64
  331.8 12.6 %all-to-all-done.13 = bf16[8,4,64,128]{3,2,1,0:T(8,128)(2,1)S(1)} async-done(((bf16[8,4,64,128]{3,2,1,0:T(8,128)(2,1)}), bf16[8,4,64,128]{3,2,1,0:T(8,128)(2,1)S(1)}, u32[]{:S(2)}, u32[]{:S(2)}) %all-to-all-start.13) | async-done | bytes 524320 | tf_op jit(solution)/shard_map/all_to_all | solution.py:60
  344.4 10.2 %all-to-all-start.17 = ((bf16[4,64,128]{2,1,0:T(8,128)(2,1)}), bf16[4,64,128]{2,1,0:T(8,128)(2,1)S(1)}, u32[]{:S(2)}, u32[]{:S(2)}) async-start(bf16[4,64,128]{2,1,0:T(8,128)(2,1)} %reduce_sum.100), calls=%async_computation.17 | async-start | bytes 131072 | tf_op jit(solution)/shard_map/all_to_all | solution.py:64
  357.0 9.1 %row_terms.5 = bf16[16,64,128]{2,1,0:T(8,128)(2,1)} custom-call(s32[152]{0:T(256)S(1)} %get-tuple-element.7.refs_0_, s32[152]{0:T(256)S(1)} %broadcast_select_fusion.1.refs_1_, bf16[32,64,128]{2,1,0:T(8,128)(2,1)S(1)} %bitcast.18, bf16[152,128,128]{2,1,0:T(8,128)(2,1)S(1)} %bitcast.16), custom_call_target="tpu_custom_call" | custom-call | flops 318767104 | bytes 4980736 | tf_op jit(solution)/shard_map/row_terms/pallas_call | solution.py:44
  367.6 6.9 %all-to-all-start.14 = ((bf16[16,64,128]{2,1,0:T(8,128)(2,1)}), bf16[16,64,128]{2,1,0:T(8,128)(2,1)S(1)}, u32[]{:S(2)}, u32[]{:S(2)}) async-start(bf16[16,64,128]{2,1,0:T(8,128)(2,1)} %row_terms.5), calls=%async_computation.14 | async-start | bytes 524288 | tf_op jit(solution)/shard_map/all_to_all | solution.py:64
  374.6 6.4 %collective-permute-start.5 = (bf16[64,128]{1,0:T(8,128)(2,1)S(1)}, bf16[64,128]{1,0:T(8,128)(2,1)S(1)}, u32[]{:S(2)}, u32[]{:S(2)}) collective-permute-start(bf16[64,128]{1,0:T(8,128)(2,1)S(1)} %reduce_sum.101), channel_id=1, source_target_pairs={{0,0},{1,16},{2,32},{3,48},{4,64},{5,80},{6,96},{7,112},{8,128},{9... | collective-permute-start | bytes 49160 | tf_op jit(solution)/shard_map/ppermute | solution.py:91
  381.1 10.3 %collective-permute-done.5 = bf16[64,128]{1,0:T(8,128)(2,1)S(1)} collective-permute-done((bf16[64,128]{1,0:T(8,128)(2,1)S(1)}, bf16[64,128]{1,0:T(8,128)(2,1)S(1)}, u32[]{:S(2)}, u32[]{:S(2)}) %collective-permute-start.5) | collective-permute-done | bytes 16416 | tf_op jit(solution)/shard_map/ppermute | solution.py:91
  (63 shorter events, 65.3 us)
Async XLA Ops:
  0.0 80.4 %copy-start.7 = (s32[1,1,152]{2,1,0:T(1,128)S(1)}, s32[1,1,152]{2,1,0:T(1,128)}, u32[]{:S(2)}) copy-start(s32[1,1,152]{2,1,0:T(1,128)} %param.7) | copy-start | bytes 1828
  0.8 16.7 %collective-permute-start = (bf16[64,128]{1,0:T(8,128)(2,1)S(1)}, bf16[64,128]{1,0:T(8,128)(2,1)S(1)}, u32[]{:S(2)}, u32[]{:S(2)}) collective-permute-start(bf16[64,128]{1,0:T(8,128)(2,1)S(1)} %convert_element_type.70), channel_id=1, source_target_pairs={{0,0},{1,16},{2,32},{3,48},{4,64},{5,80},{6,96},{7,112},{8,128},{9... | collective-permute-start | bytes 49160 | tf_op jit(solution)/shard_map/ppermute | solution.py:91
  58.1 18.6 %all-to-all-start.1 = ((bf16[8,4,64,128]{3,2,1,0:T(8,128)(2,1)}), bf16[8,4,64,128]{3,2,1,0:T(8,128)(2,1)S(1)}, u32[]{:S(2)}, u32[]{:S(2)}) async-start(bf16[8,4,64,128]{3,2,1,0:T(8,128)(2,1)} %broadcast_in_dim.25), calls=%async_computation.1 | async-start | bytes 1048576 | tf_op jit(solution)/shard_map/all_to_all | solution.py:60
  63.0 2.4 copy-start
  65.4 0.7 copy-start.6
  74.1 70.8 %copy-start.8 = (f32[64,128]{1,0:T(8,128)S(1)}, f32[64,128]{1,0:T(8,128)}, u32[]{:S(2)}) copy-start(f32[64,128]{1,0:T(8,128)} %param.5) | copy-start | bytes 98308
  76.8 18.3 %all-to-all-start.4 = ((bf16[8,4,64,128]{3,2,1,0:T(8,128)(2,1)}), bf16[8,4,64,128]{3,2,1,0:T(8,128)(2,1)S(1)}, u32[]{:S(2)}, u32[]{:S(2)}) async-start(bf16[8,4,64,128]{3,2,1,0:T(8,128)(2,1)} %bitcast.5), calls=%async_computation.4 | async-start | bytes 1048576 | tf_op jit(solution)/shard_map/all_to_all | solution.py:64
  80.4 2.4 copy-start.1
  95.1 12.2 %all-to-all-start.2 = ((bf16[16,64,128]{2,1,0:T(8,128)(2,1)}), bf16[16,64,128]{2,1,0:T(8,128)(2,1)S(1)}, u32[]{:S(2)}, u32[]{:S(2)}) async-start(bf16[16,64,128]{2,1,0:T(8,128)(2,1)} %row_terms.3), calls=%async_computation.2 | async-start | bytes 524288 | tf_op jit(solution)/shard_map/all_to_all | solution.py:64
  107.3 16.4 %all-to-all-start.5 = ((bf16[4,64,128]{2,1,0:T(8,128)(2,1)}), bf16[4,64,128]{2,1,0:T(8,128)(2,1)S(1)}, u32[]{:S(2)}, u32[]{:S(2)}) async-start(bf16[4,64,128]{2,1,0:T(8,128)(2,1)} %reduce_sum.94), calls=%async_computation.5 | async-start | bytes 131072 | tf_op jit(solution)/shard_map/all_to_all | solution.py:64
  110.7 17.4 %collective-permute-start.2 = (bf16[64,128]{1,0:T(8,128)(2,1)S(1)}, bf16[64,128]{1,0:T(8,128)(2,1)S(1)}, u32[]{:S(2)}, u32[]{:S(2)}) collective-permute-start(bf16[64,128]{1,0:T(8,128)(2,1)S(1)} %convert_element_type.77), channel_id=1, source_target_pairs={{0,0},{1,16},{2,32},{3,48},{4,64},{5,80},{6,96},{7,112},{8,128},{9... | collective-permute-start | bytes 49160 | tf_op jit(solution)/shard_map/ppermute | solution.py:91
  128.1 16.7 %collective-permute-start.1 = (bf16[64,128]{1,0:T(8,128)(2,1)S(1)}, bf16[64,128]{1,0:T(8,128)(2,1)S(1)}, u32[]{:S(2)}, u32[]{:S(2)}) collective-permute-start(bf16[64,128]{1,0:T(8,128)(2,1)S(1)} %get-tuple-element.11), channel_id=1, source_target_pairs={{0,0},{1,16},{2,32},{3,48},{4,64},{5,80},{6,96},{7,112},{8,128},{9... | collective-permute-start | bytes 49160 | tf_op jit(solution)/shard_map/ppermute | solution.py:91
  157.3 24.5 %all-to-all-start.9 = ((bf16[4,64,128]{2,1,0:T(8,128)(2,1)}), bf16[4,64,128]{2,1,0:T(8,128)(2,1)S(1)}, u32[]{:S(2)}, u32[]{:S(2)}) async-start(bf16[4,64,128]{2,1,0:T(8,128)(2,1)} %broadcast_in_dim.28), calls=%async_computation.9 | async-start | bytes 131072 | tf_op jit(solution)/shard_map/all_to_all | solution.py:60
  168.7 2.4 copy-start.2
  198.8 17.7 %all-to-all-start.10 = ((bf16[8,4,64,128]{3,2,1,0:T(8,128)(2,1)}), bf16[8,4,64,128]{3,2,1,0:T(8,128)(2,1)S(1)}, u32[]{:S(2)}, u32[]{:S(2)}) async-start(bf16[8,4,64,128]{3,2,1,0:T(8,128)(2,1)} %broadcast_in_dim.29), calls=%async_computation.10 | async-start | bytes 1048576 | tf_op jit(solution)/shard_map/all_to_all | solution.py:60
  216.5 22.6 %all-to-all-start.8 = ((bf16[4,64,128]{2,1,0:T(8,128)(2,1)}), bf16[4,64,128]{2,1,0:T(8,128)(2,1)S(1)}, u32[]{:S(2)}, u32[]{:S(2)}) async-start(bf16[4,64,128]{2,1,0:T(8,128)(2,1)} %reduce_sum.96), calls=%async_computation.8 | async-start | bytes 131072 | tf_op jit(solution)/shard_map/all_to_all | solution.py:64
  226.1 2.4 copy-start.3
  239.2 13.7 %all-to-all-start.11 = ((bf16[16,64,128]{2,1,0:T(8,128)(2,1)}), bf16[16,64,128]{2,1,0:T(8,128)(2,1)S(1)}, u32[]{:S(2)}, u32[]{:S(2)}) async-start(bf16[16,64,128]{2,1,0:T(8,128)(2,1)} %row_terms.4), calls=%async_computation.11 | async-start | bytes 524288 | tf_op jit(solution)/shard_map/all_to_all | solution.py:64
  246.4 16.7 %collective-permute-start.4 = (bf16[64,128]{1,0:T(8,128)(2,1)S(1)}, bf16[64,128]{1,0:T(8,128)(2,1)S(1)}, u32[]{:S(2)}, u32[]{:S(2)}) collective-permute-start(bf16[64,128]{1,0:T(8,128)(2,1)S(1)} %convert_element_type.86), channel_id=1, source_target_pairs={{0,0},{1,16},{2,32},{3,48},{4,64},{5,80},{6,96},{7,112},{8,128},{9... | collective-permute-start | bytes 49160 | tf_op jit(solution)/shard_map/ppermute | solution.py:91
  263.9 23.7 %all-to-all-start.15 = ((bf16[16,64,128]{2,1,0:T(8,128)(2,1)}), bf16[16,64,128]{2,1,0:T(8,128)(2,1)S(1)}, u32[]{:S(2)}, u32[]{:S(2)}) async-start(bf16[16,64,128]{2,1,0:T(8,128)(2,1)} %broadcast_in_dim.32), calls=%async_computation.15 | async-start | bytes 524288 | tf_op jit(solution)/shard_map/all_to_all | solution.py:60
  270.8 16.7 %collective-permute-start.3 = (bf16[64,128]{1,0:T(8,128)(2,1)S(1)}, bf16[64,128]{1,0:T(8,128)(2,1)S(1)}, u32[]{:S(2)}, u32[]{:S(2)}) collective-permute-start(bf16[64,128]{1,0:T(8,128)(2,1)S(1)} %get-tuple-element.9), channel_id=1, source_target_pairs={{0,0},{1,16},{2,32},{3,48},{4,64},{5,80},{6,96},{7,112},{8,128},{9... | collective-permute-start | bytes 49160 | tf_op jit(solution)/shard_map/ppermute | solution.py:91
  288.2 23.7 %all-to-all-start.12 = ((bf16[4,64,128]{2,1,0:T(8,128)(2,1)}), bf16[4,64,128]{2,1,0:T(8,128)(2,1)S(1)}, u32[]{:S(2)}, u32[]{:S(2)}) async-start(bf16[4,64,128]{2,1,0:T(8,128)(2,1)} %broadcast_in_dim.30), calls=%async_computation.12 | async-start | bytes 131072 | tf_op jit(solution)/shard_map/all_to_all | solution.py:60
  298.9 2.4 copy-start.4
  327.5 16.9 %all-to-all-start.13 = ((bf16[8,4,64,128]{3,2,1,0:T(8,128)(2,1)}), bf16[8,4,64,128]{3,2,1,0:T(8,128)(2,1)S(1)}, u32[]{:S(2)}, u32[]{:S(2)}) async-start(bf16[8,4,64,128]{3,2,1,0:T(8,128)(2,1)} %broadcast_in_dim.31), calls=%async_computation.13 | async-start | bytes 1048576 | tf_op jit(solution)/shard_map/all_to_all | solution.py:60
  344.4 23.2 %all-to-all-start.17 = ((bf16[4,64,128]{2,1,0:T(8,128)(2,1)}), bf16[4,64,128]{2,1,0:T(8,128)(2,1)S(1)}, u32[]{:S(2)}, u32[]{:S(2)}) async-start(bf16[4,64,128]{2,1,0:T(8,128)(2,1)} %reduce_sum.100), calls=%async_computation.17 | async-start | bytes 131072 | tf_op jit(solution)/shard_map/all_to_all | solution.py:64
  354.6 2.4 copy-start.5
  367.6 13.4 %all-to-all-start.14 = ((bf16[16,64,128]{2,1,0:T(8,128)(2,1)}), bf16[16,64,128]{2,1,0:T(8,128)(2,1)S(1)}, u32[]{:S(2)}, u32[]{:S(2)}) async-start(bf16[16,64,128]{2,1,0:T(8,128)(2,1)} %row_terms.5), calls=%async_computation.14 | async-start | bytes 524288 | tf_op jit(solution)/shard_map/all_to_all | solution.py:64
  374.6 16.7 %collective-permute-start.5 = (bf16[64,128]{1,0:T(8,128)(2,1)S(1)}, bf16[64,128]{1,0:T(8,128)(2,1)S(1)}, u32[]{:S(2)}, u32[]{:S(2)}) collective-permute-start(bf16[64,128]{1,0:T(8,128)(2,1)S(1)} %reduce_sum.101), channel_id=1, source_target_pairs={{0,0},{1,16},{2,32},{3,48},{4,64},{5,80},{6,96},{7,112},{8,128},{9... | collective-permute-start | bytes 49160 | tf_op jit(solution)/shard_map/ppermute | solution.py:91

commit v2 on v1

v2 whole, which is shorter than its diff:
```python
import jax
import jax.numpy as jnp
from jax import lax
from jax.experimental import pallas as pl
from jax.experimental.pallas import tpu as pltpu
from jax.sharding import Mesh, PartitionSpec as P

CENTER = 0.25
HALF_WIDTH = 2.0
DEGREE = 3
CHUNKS = 8
ROW = ("zh", "zl", "xl")
COL = ("xh", "y", "core")
PLANE = ("xl",) + COL
ALL = ROW + COL
N_ZH, N_ZL, N_XL, N_COL = 4, 4, 2, 16
N_HALF = N_ZH * N_ZL * N_XL // N_COL
VMEM = pl.BlockSpec(memory_space=pltpu.VMEM)
SMEM = pl.BlockSpec(memory_space=pltpu.SMEM)
FLOAT = jnp.float32
WIRE = jnp.bfloat16
SMALL, LARGE = 4 << 20, 16 << 20


def places():
    for h in range(N_HALF):
        for b in range(N_COL):
            z, parity = divmod(h * N_COL + b, N_XL)
            yield h, b, z % N_ZL, z // N_ZL, parity


def terms_kernel(rows, cols, row_targets, col_targets, x_ref, blocks, out_ref, col_acc, row_acc):
    slots = blocks.shape[0]
    part = slots // CHUNKS
    width = x_ref.shape[0] * x_ref.shape[3]
    half = x_ref.shape[3]
    col_acc[...] = jnp.zeros_like(col_acc)
    row_acc[...] = jnp.zeros_like(row_acc)

    def chunk(i, carry):
        base = i * part
        for u in range(part):
            s = base + u
            block = blocks[s]
            col = cols[s]
            x_row = x_ref[:, rows[s], N_HALF].reshape(width, block.shape[0])
            x_col = x_ref[:, lax.rem(col, N_COL), lax.div(col, N_COL)].reshape(width, block.shape[0])
            t = col_targets[s]
            col_acc[t] = col_acc[t] + lax.dot_general(x_row, block, (((1,), (0,)), ((), ())), preferred_element_type=FLOAT)
            t = row_targets[s]
            row_acc[t] = row_acc[t] + lax.dot_general(x_col, block, (((1,), (1,)), ((), ())), preferred_element_type=FLOAT)
        return carry

    lax.fori_loop(0, CHUNKS, chunk, 0)
    for k in range(x_ref.shape[0]):
        lines = slice(k * half, (k + 1) * half)
        for h in range(N_HALF):
            out_ref[k, :, h] = col_acc[h * N_COL : (h + 1) * N_COL, lines].astype(WIRE)
        out_ref[k, :, N_HALF] = row_acc[:N_COL, lines].astype(WIRE)


def terms(x, blocks, indices):
    slots, size = blocks.shape[:2]
    width = x.shape[0] * x.shape[3]
    return pl.pallas_call(
        terms_kernel,
        out_shape=jax.ShapeDtypeStruct(x.shape, WIRE),
        in_specs=[SMEM] * 4 + [VMEM, VMEM],
        out_specs=VMEM,
        scratch_shapes=[
            pltpu.VMEM((N_HALF * N_COL + 1, width, size), FLOAT),
            pltpu.VMEM((N_COL + 1, width, size), FLOAT),
        ],
        compiler_params=pltpu.CompilerParams(vmem_limit_bytes=LARGE),
        name="terms",
    )(*indices, x, blocks)


def merge_kernel(got_ref, out_ref, acc):
    for h, b, zl, zh, parity in places():
        acc[zl, zh, parity] = got_ref[0, b, h].astype(FLOAT) + got_ref[1, b, h].astype(FLOAT)
    zh, zl = lax.axis_index("zh"), lax.axis_index("zl")
    for parity in range(N_XL):
        total = got_ref[parity, 0, N_HALF].astype(FLOAT)
        for b in range(1, N_COL):
            total = total + got_ref[parity, b, N_HALF].astype(FLOAT)
        acc[zl, zh, parity] = acc[zl, zh, parity] + total
    out_ref[...] = acc[...].astype(WIRE)


def merge(got):
    shape = (N_ZL, N_ZH, N_XL) + got.shape[3:]
    return pl.pallas_call(
        merge_kernel,
        out_shape=jax.ShapeDtypeStruct(shape, WIRE),
        in_specs=[VMEM],
        out_specs=VMEM,
        scratch_shapes=[pltpu.VMEM(shape, FLOAT)],
        compiler_params=pltpu.CompilerParams(vmem_limit_bytes=SMALL),
        name="merge",
    )(got)


def deal_kernel(all_ref, out_ref):
    zh, zl = lax.axis_index("zh"), lax.axis_index("zl")
    for h, b, b_zl, b_zh, parity in places():
        piece = all_ref[b_zl, b_zh, parity]
        for xl in range(N_XL):
            out_ref[xl, b, h] = piece
    for xl in range(N_XL):
        piece = all_ref[zl, zh, xl]
        for b in range(N_COL):
            out_ref[xl, b, N_HALF] = piece


def deal(pieces):
    return pl.pallas_call(
        deal_kernel,
        out_shape=jax.ShapeDtypeStruct((N_XL, N_COL, N_HALF + 1) + pieces.shape[3:], WIRE),
        in_specs=[VMEM],
        out_specs=VMEM,
        compiler_params=pltpu.CompilerParams(vmem_limit_bytes=SMALL),
        name="deal",
    )(pieces)


def exchange(x, axes):
    return lax.all_to_all(x, axes, 0, 0, tiled=True)


def total(x):
    return jnp.sum(x.astype(FLOAT), axis=0)


def local(vectors, blocks, slot_block_rows, slot_block_columns, counts):
    width, size = vectors.shape
    blocks = blocks[0, 0]
    rows = slot_block_rows[0, 0]
    cols = slot_block_columns[0, 0]
    slots = blocks.shape[0]
    row, col = lax.axis_index(ROW), lax.axis_index(COL)
    zh = lax.axis_index("zh")
    xl = lax.axis_index("xl")
    global_rows = row * N_COL + rows
    global_cols = (col + N_COL * (cols // N_COL)) * N_COL + cols % N_COL
    live = (jnp.arange(slots, dtype=jnp.int32) < counts[0, 0]) & (global_rows <= global_cols)
    indices = (rows, cols, jnp.where(live, rows, N_COL), jnp.where(live, cols, N_HALF * N_COL))

    def plane_sums(now):
        wire = now.astype(WIRE)
        pieces = exchange(jnp.broadcast_to(wire[None], (N_ZL,) + wire.shape), "zl")
        got = exchange(deal(pieces).reshape(N_XL * N_COL, N_HALF + 1, *wire.shape[2:]), PLANE)
        out = terms(got.reshape(N_XL, N_COL, *got.shape[1:]), blocks, indices)
        got = exchange(out.reshape(got.shape), PLANE).reshape(out.shape)
        return total(exchange(merge(got), "zl")).astype(WIRE)

    halves = lax.all_gather(vectors.reshape(N_XL, width // N_XL, size), "xl")[:, xl]
    before, now = None, lax.all_gather(halves, "zh")
    for step in range(DEGREE - 1):
        image = total(lax.all_gather(plane_sums(now), "zh"))
        after = (image - CENTER * now) / HALF_WIDTH
        if step > 0:
            after = 2.0 * (image - CENTER * now) / HALF_WIDTH - before
        before, now = now, after
    image = total(exchange(plane_sums(now), "zh"))
    own = 2.0 * (image - CENTER * now[zh]) / HALF_WIDTH - before[zh]
    return lax.all_gather(own, "xl")[:, xl].reshape(width, size)


def solution(mesh):
    split = Mesh(mesh.devices.reshape(N_ZH, N_ZL, N_XL, 2, 4, 2), ALL)
    in_specs = (
        P(None, ALL),
        P(ROW, COL, None, None, None),
        P(ROW, COL, None),
        P(ROW, COL, None),
        P(ROW, COL),
    )
    return jax.shard_map(local, mesh=split, in_specs=in_specs, out_specs=P(None, ALL), check_vma=False)
```

time: 394 us -> 302 us (0.77)
  the two profiles are of different devices: /device:TPU:28 before, /device:TPU:2 now
where the time goes in v2:
time: 302 us
  blocking collectives  232 us (77%)
  waiting for transfers between devices  23.6 us (8%)
  Pallas kernels  19.2 us (6%)
  starting transfers between devices  14.3 us (5%)
  local copies, waits for them, and re-layouts  9.36 us (3%)
    all_to_all x11, blocking collectives, exchange(): return lax.all_to_all(x, axes, 0, 0, tiled=True)  155 us
    all_gather x2, blocking collectives, local(): image = total(lax.all_gather(plane_sums(now), 'zh'))  41.3 us
    all_to_all x2, waiting for transfers between devices, exchange(): return lax.all_to_all(x, axes, 0, 0, tiled=True)  23.6 us
    all_gather x1, blocking collectives, local(): before, now = (None, lax.all_gather(halves, 'zh'))  22 us
    pallas_call x3, Pallas kernels, terms(): pl.pallas_call(terms_kernel, out_shape=jax.ShapeDtypeStruct(x.shape, WIRE...  17.7 us
    all_to_all x2, starting transfers between devices, exchange(): return lax.all_to_all(x, axes, 0, 0, tiled=True)  14.3 us
    all_gather x1, blocking collectives, local(): lax.all_gather(vectors.reshape(N_XL, width // N_XL, size), 'xl')[:, xl]  8.72 us
    unnamed x14, local copies, waits for them, and re-layouts  8.61 us
  transfers between devices with their start and end apart: 2, of which 2 were waited for; matrix products, arithmetic and copies ran while one was open for 0% of the time, Pallas kernels for 0%

profile of v2, /device:TPU:2, one launch (start us, length us, event | category | flops | bytes accessed | tf_op | source)
XLA Modules:
  0.0 301.5 jit_solution(8166389394458459285)
XLA Ops:
  0.0 8.7 %all_gather.22 = f32[2,2,32,128]{3,2,1,0:T(8,128)S(1)} all-gather(f32[1,2,32,128]{3,2,1,0:T(8,128)} %bitcast.68), channel_id=1, replica_groups=mesh['zh'=4,'zl'=4,'xl'=2,'xh'=2,'y'=4,'core'=2] {'xl'}, dimensions={0}, use_global_device_ids=true | all-gather | bytes 98304 | tf_op jit(solution)/shard_map/all_gather | solution.py:157
  8.7 22.0 %all-gather = f32[8,1,32,128]{3,2,1,0:T(8,128)S(1)} all-gather(f32[2,1,32,128]{3,2,1,0:T(8,128)S(1)} %constant_dynamic-slice_fusion.1), channel_id=2, replica_groups=mesh['zh'=4,'zl'=4,'xl'=2,'xh'=2,'y'=4,'core'=2] {'zh'}, dimensions={0}, use_global_device_ids=true | all-gather | bytes 163840 | tf_op jit(solution)/shard_map/all_gather | solution.py:158
  30.8 10.1 %all_to_all.65.all_ref = bf16[4,4,2,32,128]{4,3,2,1,0:T(8,128)(2,1)S(1)} all-to-all(bf16[4,4,2,32,128]{4,3,2,1,0:T(8,128)(2,1)S(1)} %broadcast_in_dim.12), channel_id=1, replica_groups=mesh['zh'=4,'zl'=4,'xl'=2,'xh'=2,'y'=4,'core'=2] {'zl'}, dimensions={0} | all-to-all | bytes 524288 | tf_op jit(solution)/shard_map/all_to_all | solution.py:128
  40.9 1.0 deal.3
  41.9 7.6 %all-to-all-start.1 = ((bf16[32,3,32,128]{3,2,1,0:T(8,128)(2,1)}), bf16[32,3,32,128]{3,2,1,0:T(8,128)(2,1)S(1)}, u32[]{:S(2)}, u32[]{:S(2)}) async-start(bf16[32,3,32,128]{3,2,1,0:T(8,128)(2,1)} %bitcast.5), calls=%async_computation.1 | async-start | bytes 1572864 | tf_op jit(solution)/shard_map/all_to_all | solution.py:128
  50.2 0.7 broadcast_select_fusion
  50.9 0.7 broadcast_select_fusion.1.row_targets
  51.6 10.6 %all-to-all-done.1 = bf16[32,3,32,128]{3,2,1,0:T(8,128)(2,1)S(1)} async-done(((bf16[32,3,32,128]{3,2,1,0:T(8,128)(2,1)}), bf16[32,3,32,128]{3,2,1,0:T(8,128)(2,1)S(1)}, u32[]{:S(2)}, u32[]{:S(2)}) %all-to-all-start.1) | async-done | bytes 786464 | tf_op jit(solution)/shard_map/all_to_all | solution.py:128
  62.2 2.4 copy-done
  64.7 0.7 copy-done.3
  65.3 0.7 copy-done.5
  66.0 5.9 %terms.3 = bf16[2,16,3,32,128]{4,3,2,1,0:T(8,128)(2,1)S(1)} custom-call(s32[152]{0:T(256)S(1)} %bitcast.56, s32[152]{0:T(256)S(1)} %bitcast.60, s32[152]{0:T(256)S(1)} %broadcast_select_fusion.1.row_targets, s32[152]{0:T(256)S(1)} %get-tuple-element.9.col_targets, bf16[2,16,3,32,128]{4,3,2,1,0:T(8,128)(2,1)S(1)} %bitcast.48, bf16[152,128,128]{2,1,0:T(8,128)(2,1)S(1)} %bitcast.40), custom_call_target="tpu_custom_call" | custom-call | tf_op jit(solution)/shard_map/terms/pallas_call | solution.py:65
  71.9 17.9 %all_to_all.66 = bf16[32,3,32,128]{3,2,1,0:T(8,128)(2,1)S(1)} all-to-all(bf16[32,3,32,128]{3,2,1,0:T(8,128)(2,1)S(1)} %bitcast.51), channel_id=1, replica_groups=mesh['zh'=4,'zl'=4,'xl'=2,'xh'=2,'y'=4,'core'=2] {'xl','xh','y','core'}, dimensions={0} | all-to-all | bytes 1572864 | tf_op jit(solution)/shard_map/all_to_all | solution.py:128
  90.0 12.7 %all_to_all.67 = bf16[4,4,2,32,128]{4,3,2,1,0:T(8,128)(2,1)S(1)} all-to-all(bf16[4,4,2,32,128]{4,3,2,1,0:T(8,128)(2,1)S(1)} %merge.3), channel_id=1, replica_groups=mesh['zh'=4,'zl'=4,'xl'=2,'xh'=2,'y'=4,'core'=2] {'zl'}, dimensions={0} | all-to-all | bytes 524288 | tf_op jit(solution)/shard_map/all_to_all | solution.py:128
  102.7 20.5 %all-gather.1 = bf16[16,2,32,128]{3,2,1,0:T(8,128)(2,1)S(1)} all-gather(bf16[4,2,32,128]{3,2,1,0:T(8,128)(2,1)S(1)} %reduce_sum.65), channel_id=3, replica_groups=mesh['zh'=4,'zl'=4,'xl'=2,'xh'=2,'y'=4,'core'=2] {'zh'}, dimensions={0}, use_global_device_ids=true | all-gather | bytes 327680 | tf_op jit(solution)/shard_map/all_gather | solution.py:160
  123.3 9.5 %all_to_all.68.all_ref = bf16[4,4,2,32,128]{4,3,2,1,0:T(8,128)(2,1)S(1)} all-to-all(bf16[4,4,2,32,128]{4,3,2,1,0:T(8,128)(2,1)S(1)} %broadcast_in_dim.13), channel_id=1, replica_groups=mesh['zh'=4,'zl'=4,'xl'=2,'xh'=2,'y'=4,'core'=2] {'zl'}, dimensions={0} | all-to-all | bytes 524288 | tf_op jit(solution)/shard_map/all_to_all | solution.py:128
  133.0 17.3 %all_to_all.69 = bf16[32,3,32,128]{3,2,1,0:T(8,128)(2,1)S(1)} all-to-all(bf16[32,3,32,128]{3,2,1,0:T(8,128)(2,1)S(1)} %bitcast.44), channel_id=1, replica_groups=mesh['zh'=4,'zl'=4,'xl'=2,'xh'=2,'y'=4,'core'=2] {'xl','xh','y','core'}, dimensions={0} | all-to-all | bytes 1572864 | tf_op jit(solution)/shard_map/all_to_all | solution.py:128
  150.3 2.4 copy-done.1
  152.7 5.9 %terms.4 = bf16[2,16,3,32,128]{4,3,2,1,0:T(8,128)(2,1)S(1)} custom-call(s32[152]{0:T(256)S(1)} %bitcast.57, s32[152]{0:T(256)S(1)} %bitcast.61, s32[152]{0:T(256)S(1)} %broadcast_select_fusion.1.row_targets, s32[152]{0:T(256)S(1)} %get-tuple-element.9.col_targets, bf16[2,16,3,32,128]{4,3,2,1,0:T(8,128)(2,1)S(1)} %bitcast.52, bf16[152,128,128]{2,1,0:T(8,128)(2,1)S(1)} %bitcast.41), custom_call_target="tpu_custom_call" | custom-call | tf_op jit(solution)/shard_map/terms/pallas_call | solution.py:65
  158.6 17.9 %all_to_all.70 = bf16[32,3,32,128]{3,2,1,0:T(8,128)(2,1)S(1)} all-to-all(bf16[32,3,32,128]{3,2,1,0:T(8,128)(2,1)S(1)} %bitcast.53), channel_id=1, replica_groups=mesh['zh'=4,'zl'=4,'xl'=2,'xh'=2,'y'=4,'core'=2] {'xl','xh','y','core'}, dimensions={0} | all-to-all | bytes 1572864 | tf_op jit(solution)/shard_map/all_to_all | solution.py:128
  176.6 12.6 %all_to_all.71 = bf16[4,4,2,32,128]{4,3,2,1,0:T(8,128)(2,1)S(1)} all-to-all(bf16[4,4,2,32,128]{4,3,2,1,0:T(8,128)(2,1)S(1)} %merge.4), channel_id=1, replica_groups=mesh['zh'=4,'zl'=4,'xl'=2,'xh'=2,'y'=4,'core'=2] {'zl'}, dimensions={0} | all-to-all | bytes 524288 | tf_op jit(solution)/shard_map/all_to_all | solution.py:128
  189.3 20.8 %all-gather.2 = bf16[16,2,32,128]{3,2,1,0:T(8,128)(2,1)S(1)} all-gather(bf16[4,2,32,128]{3,2,1,0:T(8,128)(2,1)S(1)} %reduce_sum.67), channel_id=4, replica_groups=mesh['zh'=4,'zl'=4,'xl'=2,'xh'=2,'y'=4,'core'=2] {'zh'}, dimensions={0}, use_global_device_ids=true | all-gather | bytes 327680 | tf_op jit(solution)/shard_map/all_gather | solution.py:160
  210.2 9.5 %all_to_all.72.all_ref = bf16[4,4,2,32,128]{4,3,2,1,0:T(8,128)(2,1)S(1)} all-to-all(bf16[4,4,2,32,128]{4,3,2,1,0:T(8,128)(2,1)S(1)} %broadcast_in_dim.26), channel_id=1, replica_groups=mesh['zh'=4,'zl'=4,'xl'=2,'xh'=2,'y'=4,'core'=2] {'zl'}, dimensions={0} | all-to-all | bytes 524288 | tf_op jit(solution)/shard_map/all_to_all | solution.py:128
  219.8 17.1 %all_to_all.73 = bf16[32,3,32,128]{3,2,1,0:T(8,128)(2,1)S(1)} all-to-all(bf16[32,3,32,128]{3,2,1,0:T(8,128)(2,1)S(1)} %bitcast.46), channel_id=1, replica_groups=mesh['zh'=4,'zl'=4,'xl'=2,'xh'=2,'y'=4,'core'=2] {'xl','xh','y','core'}, dimensions={0} | all-to-all | bytes 1572864 | tf_op jit(solution)/shard_map/all_to_all | solution.py:128
  236.9 2.4 copy-done.2
  239.3 5.9 %terms.5 = bf16[2,16,3,32,128]{4,3,2,1,0:T(8,128)(2,1)S(1)} custom-call(s32[152]{0:T(256)S(1)} %bitcast.58, s32[152]{0:T(256)S(1)} %bitcast.62, s32[152]{0:T(256)S(1)} %broadcast_select_fusion.1.row_targets, s32[152]{0:T(256)S(1)} %get-tuple-element.9.col_targets, bf16[2,16,3,32,128]{4,3,2,1,0:T(8,128)(2,1)S(1)} %bitcast.49, bf16[152,128,128]{2,1,0:T(8,128)(2,1)S(1)} %bitcast.42), custom_call_target="tpu_custom_call" | custom-call | tf_op jit(solution)/shard_map/terms/pallas_call | solution.py:65
  245.2 17.9 %all_to_all.74 = bf16[32,3,32,128]{3,2,1,0:T(8,128)(2,1)S(1)} all-to-all(bf16[32,3,32,128]{3,2,1,0:T(8,128)(2,1)S(1)} %bitcast.50), channel_id=1, replica_groups=mesh['zh'=4,'zl'=4,'xl'=2,'xh'=2,'y'=4,'core'=2] {'xl','xh','y','core'}, dimensions={0} | all-to-all | bytes 1572864 | tf_op jit(solution)/shard_map/all_to_all | solution.py:128
  263.3 12.6 %all_to_all.75 = bf16[4,4,2,32,128]{4,3,2,1,0:T(8,128)(2,1)S(1)} all-to-all(bf16[4,4,2,32,128]{4,3,2,1,0:T(8,128)(2,1)S(1)} %merge.5), channel_id=1, replica_groups=mesh['zh'=4,'zl'=4,'xl'=2,'xh'=2,'y'=4,'core'=2] {'zl'}, dimensions={0} | all-to-all | bytes 524288 | tf_op jit(solution)/shard_map/all_to_all | solution.py:128
  275.9 0.7 reduce_sum.69
  276.6 6.7 %all-to-all-start.12 = ((bf16[4,2,32,128]{3,2,1,0:T(8,128)(2,1)}), bf16[4,2,32,128]{3,2,1,0:T(8,128)(2,1)S(1)}, u32[]{:S(2)}, u32[]{:S(2)}) async-start(bf16[4,2,32,128]{3,2,1,0:T(8,128)(2,1)} %reduce_sum.69), calls=%async_computation.12 | async-start | bytes 131072 | tf_op jit(solution)/shard_map/all_to_all | solution.py:128
  283.2 13.0 %all-to-all-done.12 = bf16[4,2,32,128]{3,2,1,0:T(8,128)(2,1)S(1)} async-done(((bf16[4,2,32,128]{3,2,1,0:T(8,128)(2,1)}), bf16[4,2,32,128]{3,2,1,0:T(8,128)(2,1)S(1)}, u32[]{:S(2)}, u32[]{:S(2)}) %all-to-all-start.12) | async-done | bytes 65568 | tf_op jit(solution)/shard_map/all_to_all | solution.py:128
  296.3 4.6 %all_gather.28 = f32[2,2,32,128]{3,2,1,0:T(8,128)S(1)} all-gather(f32[1,2,32,128]{3,2,1,0:T(8,128)S(1)} %fusion.1), channel_id=1, replica_groups=mesh['zh'=4,'zl'=4,'xl'=2,'xh'=2,'y'=4,'core'=2] {'xl'}, dimensions={0}, use_global_device_ids=true | all-gather | bytes 98304 | tf_op jit(solution)/shard_map/all_gather | solution.py:167
  (28 shorter events, 1.6 us)
Async XLA Ops:
  41.9 20.3 %all-to-all-start.1 = ((bf16[32,3,32,128]{3,2,1,0:T(8,128)(2,1)}), bf16[32,3,32,128]{3,2,1,0:T(8,128)(2,1)S(1)}, u32[]{:S(2)}, u32[]{:S(2)}) async-start(bf16[32,3,32,128]{3,2,1,0:T(8,128)(2,1)} %bitcast.5), calls=%async_computation.1 | async-start | bytes 1572864 | tf_op jit(solution)/shard_map/all_to_all | solution.py:128
  62.2 2.4 copy-start
  64.7 0.7 copy-start.3
  65.3 0.7 copy-start.5
  71.9 78.3 %copy-start.4 = (s32[1,1,152]{2,1,0:T(1,128)S(1)}, s32[1,1,152]{2,1,0:T(1,128)}, u32[]{:S(2)}) copy-start(s32[1,1,152]{2,1,0:T(1,128)} %param.7) | copy-start | bytes 1828
  71.9 78.3 %copy-start.6 = (s32[1,1,152]{2,1,0:T(1,128)S(1)}, s32[1,1,152]{2,1,0:T(1,128)}, u32[]{:S(2)}) copy-start(s32[1,1,152]{2,1,0:T(1,128)} %param.8) | copy-start | bytes 1828
  150.3 2.4 copy-start.1
  236.9 2.4 copy-start.2
  276.6 19.7 %all-to-all-start.12 = ((bf16[4,2,32,128]{3,2,1,0:T(8,128)(2,1)}), bf16[4,2,32,128]{3,2,1,0:T(8,128)(2,1)S(1)}, u32[]{:S(2)}, u32[]{:S(2)}) async-start(bf16[4,2,32,128]{3,2,1,0:T(8,128)(2,1)} %reduce_sum.69), calls=%async_computation.12 | async-start | bytes 131072 | tf_op jit(solution)/shard_map/all_to_all | solution.py:128

commit v3 on v2

v3 whole, which is shorter than its diff:
```python
import jax
import jax.numpy as jnp
from jax import lax
from jax.experimental import pallas as pl
from jax.experimental.pallas import tpu as pltpu
from jax.sharding import Mesh, PartitionSpec as P

CENTER = 0.25
HALF_WIDTH = 2.0
DEGREE = 3
CHUNKS, AHEAD = 8, 2
QUAD = ("z0", "xl")
ROW = ("zh", "z1") + QUAD
COL = ("xh", "y", "core")
UNIT = QUAD + COL
UNITS = ("z1", "zh")
ALL = ROW + COL
N_ZH, N_Z1, N_Q, N_COL = 4, 2, 4, 16
N_HALF = N_ZH * N_Z1 * N_Q // N_COL
VMEM = pl.BlockSpec(memory_space=pltpu.VMEM)
SMEM = pl.BlockSpec(memory_space=pltpu.SMEM)
FLOAT = jnp.float32
WIRE = jnp.bfloat16
SMALL, LARGE = 4 << 20, 52 << 20


def places():
    for h in range(N_HALF):
        for b in range(N_COL):
            zh, rest = divmod(h * N_COL + b, N_Z1 * N_Q)
            yield h, b, rest // N_Q, zh, rest % N_Q


def terms_kernel(index, x_ref, blocks_hbm, out_ref, col_acc, row_acc, blocks, sems):
    slots = blocks.shape[0]
    part = slots // CHUNKS
    width = x_ref.shape[0] * x_ref.shape[3]
    share = x_ref.shape[3]

    def copy(i):
        here = pl.ds(i * part, part)
        return pltpu.make_async_copy(blocks_hbm.at[here], blocks.at[here], sems.at[i])

    for i in range(AHEAD):
        copy(i).start()
    col_acc[...] = jnp.zeros_like(col_acc)
    row_acc[...] = jnp.zeros_like(row_acc)

    def chunk(i, carry):
        base = i * part
        copy(i).wait()

        @pl.when(i + AHEAD < CHUNKS)
        def _():
            copy(i + AHEAD).start()

        for u in range(part):
            s = base + u
            block = blocks[s]
            col = index[slots + s]
            x_row = x_ref[:, index[s], N_HALF].reshape(width, block.shape[0])
            x_col = x_ref[:, lax.rem(col, N_COL), lax.div(col, N_COL)].reshape(width, block.shape[0])
            t = index[3 * slots + s]
            col_acc[t] = col_acc[t] + lax.dot_general(x_row, block, (((1,), (0,)), ((), ())), preferred_element_type=FLOAT)
            t = index[2 * slots + s]
            row_acc[t] = row_acc[t] + lax.dot_general(x_col, block, (((1,), (1,)), ((), ())), preferred_element_type=FLOAT)
        return carry

    lax.fori_loop(0, CHUNKS, chunk, 0)
    for k in range(x_ref.shape[0]):
        lines = slice(k * share, (k + 1) * share)
        for h in range(N_HALF):
            out_ref[k, :, h] = col_acc[h * N_COL : (h + 1) * N_COL, lines].astype(WIRE)
        out_ref[k, :, N_HALF] = row_acc[:N_COL, lines].astype(WIRE)


def terms(x, blocks, index):
    slots, size = blocks.shape[:2]
    width = x.shape[0] * x.shape[3]
    return pl.pallas_call(
        terms_kernel,
        out_shape=jax.ShapeDtypeStruct(x.shape, WIRE),
        in_specs=[SMEM, VMEM, pl.BlockSpec(memory_space=pltpu.HBM)],
        out_specs=VMEM,
        scratch_shapes=[
            pltpu.VMEM((N_HALF * N_COL + 1, width, size), FLOAT),
            pltpu.VMEM((N_COL + 1, width, size), FLOAT),
            pltpu.VMEM(blocks.shape, WIRE),
            pltpu.SemaphoreType.DMA((CHUNKS,)),
        ],
        compiler_params=pltpu.CompilerParams(vmem_limit_bytes=LARGE),
        name="terms",
    )(index, x, blocks)


def merge_kernel(got_ref, out_ref, acc):
    for h, b, z1, zh, q in places():
        piece = got_ref[0, b, h].astype(FLOAT)
        for k in range(1, N_Q):
            piece = piece + got_ref[k, b, h].astype(FLOAT)
        acc[z1, zh, q] = piece
    zh, z1 = lax.axis_index("zh"), lax.axis_index("z1")
    for q in range(N_Q):
        piece = got_ref[q, 0, N_HALF].astype(FLOAT)
        for b in range(1, N_COL):
            piece = piece + got_ref[q, b, N_HALF].astype(FLOAT)
        acc[z1, zh, q] = acc[z1, zh, q] + piece
    out_ref[...] = acc[...].astype(WIRE)


def merge(got):
    shape = (N_Z1, N_ZH, N_Q) + got.shape[3:]
    return pl.pallas_call(
        merge_kernel,
        out_shape=jax.ShapeDtypeStruct(shape, WIRE),
        in_specs=[VMEM],
        out_specs=VMEM,
        scratch_shapes=[pltpu.VMEM(shape, FLOAT)],
        compiler_params=pltpu.CompilerParams(vmem_limit_bytes=SMALL),
        name="merge",
    )(got)


def deal_kernel(all_ref, out_ref):
    zh, z1 = lax.axis_index("zh"), lax.axis_index("z1")
    for h, b, b_z1, b_zh, b_q in places():
        piece = all_ref[b_z1, b_zh, b_q]
        for q in range(N_Q):
            out_ref[q, b, h] = piece
    for q in range(N_Q):
        piece = all_ref[z1, zh, q]
        for b in range(N_COL):
            out_ref[q, b, N_HALF] = piece


def deal(pieces):
    return pl.pallas_call(
        deal_kernel,
        out_shape=jax.ShapeDtypeStruct((N_Q, N_COL, N_HALF + 1) + pieces.shape[3:], WIRE),
        in_specs=[VMEM],
        out_specs=VMEM,
        compiler_params=pltpu.CompilerParams(vmem_limit_bytes=SMALL),
        name="deal",
    )(pieces)


def exchange(x, axes):
    return lax.all_to_all(x, axes, 0, 0, tiled=True)


def total(x):
    return jnp.sum(x.astype(FLOAT), axis=0)


def local(vectors, blocks, slot_block_rows, slot_block_columns, counts):
    width, size = vectors.shape
    blocks = blocks[0, 0]
    rows = slot_block_rows[0, 0]
    cols = slot_block_columns[0, 0]
    slots = blocks.shape[0]
    row, col = lax.axis_index(ROW), lax.axis_index(COL)
    zh, z1 = lax.axis_index("zh"), lax.axis_index("z1")
    global_rows = row * N_COL + rows
    global_cols = (col + N_COL * (cols // N_COL)) * N_COL + cols % N_COL
    live = (jnp.arange(slots, dtype=jnp.int32) < counts[0, 0]) & (global_rows <= global_cols)
    index = jnp.concatenate([rows, cols, jnp.where(live, rows, N_COL), jnp.where(live, cols, N_HALF * N_COL)])

    def unit_sums(pieces):
        got = exchange(deal(pieces).reshape(N_Q * N_COL, N_HALF + 1, *pieces.shape[3:]), UNIT)
        out = terms(got.reshape(N_Q, N_COL, *got.shape[1:]), blocks, index)
        return merge(exchange(out.reshape(got.shape), UNIT).reshape(out.shape))

    quarter = exchange(vectors.reshape(N_Q, width // N_Q, size), QUAD)
    copies = jnp.broadcast_to(quarter.astype(WIRE)[None], (N_Z1 * N_ZH,) + quarter.shape)
    wire = exchange(copies, UNITS).reshape(N_Z1, N_ZH, *quarter.shape)
    before, now = None, wire[z1].astype(FLOAT).at[zh].set(quarter)
    for step in range(DEGREE - 1):
        pair_sums = total(exchange(unit_sums(wire), "z1")).astype(WIRE)
        image = total(lax.all_gather(pair_sums, "zh"))
        after = (image - CENTER * now) / HALF_WIDTH
        if step > 0:
            after = 2.0 * (image - CENTER * now) / HALF_WIDTH - before
        before, now = now, after
        wire = lax.all_gather(now.astype(WIRE), "z1")
    sums = unit_sums(wire)
    image = total(exchange(sums.reshape(-1, *sums.shape[2:]), UNITS))
    own = 2.0 * (image - CENTER * now[zh]) / HALF_WIDTH - before[zh]
    return exchange(own, QUAD).reshape(width, size)


def solution(mesh):
    split = Mesh(mesh.devices.reshape(N_ZH, N_Z1, 2, 2, 2, 4, 2), ALL)
    in_specs = (
        P(None, ALL),
        P(ROW, COL, None, None, None),
        P(ROW, COL, None),
        P(ROW, COL, None),
        P(ROW, COL),
    )
    return jax.shard_map(local, mesh=split, in_specs=in_specs, out_specs=P(None, ALL), check_vma=False)
```

time: 302 us -> 282 us (0.934)
  blocking collectives: 232 us -> 201 us
  local copies, waits for them, and re-layouts: 9.36 us -> 0.64 us
  waiting for transfers between devices: 23.6 us -> 30.5 us
  starting transfers between devices: 14.3 us -> 19.7 us
  Pallas kernels: 19.2 us -> 24 us
    all_gather x5 -> x4, blocking collectives: 76.6 us -> 50.7 us  [the longest x2 38.9 us: local(): image = total(lax.all_gather(pair_sums, 'zh'))]
    unnamed x14 -> x3, local copies, waits for them, and re-layouts: 8.61 us -> 0.62 us
    all_to_all x2 -> x3, waiting for transfers between devices: 23.6 us -> 30.5 us  [exchange(): return lax.all_to_all(x, axes, 0, 0, tiled=True)]
    all_to_all x2 -> x3, starting transfers between devices: 14.3 us -> 19.7 us  [exchange(): return lax.all_to_all(x, axes, 0, 0, tiled=True)]
    all_to_all x11 -> x9, blocking collectives: 155 us -> 151 us  [exchange(): return lax.all_to_all(x, axes, 0, 0, tiled=True)]
    pallas_call x3, Pallas kernels: 17.7 us -> 21.9 us  [terms(): pl.pallas_call(terms_kernel, out_shape=jax.ShapeDtypeStruct(x.shape, WIRE...]
  transfers between devices with their start and end apart: 2 -> 3, of which waited for: 2 -> 3; matrix products, arithmetic and copies ran while one was open for 0% -> 1% of each run, Pallas kernels for 0% -> 0%
where the time goes in v3:
time: 282 us; the launch traced here: 281 us
  blocking collectives  201 us (71%)
  waiting for transfers between devices  30.5 us (11%)
  Pallas kernels  24 us (9%)
  starting transfers between devices  19.7 us (7%)
  other arithmetic  3.83 us (1%)
    all_to_all x9, blocking collectives, exchange(): return lax.all_to_all(x, axes, 0, 0, tiled=True)  151 us
    all_gather x2, blocking collectives, local(): image = total(lax.all_gather(pair_sums, 'zh'))  38.9 us
    all_to_all x3, waiting for transfers between devices, exchange(): return lax.all_to_all(x, axes, 0, 0, tiled=True)  30.5 us
    pallas_call x3, Pallas kernels, terms(): pl.pallas_call(terms_kernel, out_shape=jax.ShapeDtypeStruct(x.shape, WIRE...  21.9 us
    all_to_all x3, starting transfers between devices, exchange(): return lax.all_to_all(x, axes, 0, 0, tiled=True)  19.7 us
    all_gather x2, blocking collectives, local(): wire = lax.all_gather(now.astype(WIRE), 'z1')  11.8 us
  transfers between devices with their start and end apart: 3, of which 3 were waited for; matrix products, arithmetic and copies ran while one was open for 1% of the time, Pallas kernels for 0%

profile of v3, /device:TPU:2, one launch (start us, length us, event | category | flops | bytes accessed | tf_op | source)
XLA Modules:
  0.0 280.8 jit_solution(16052084652241260262)
XLA Ops:
  0.0 12.5 %all_to_all.60 = f32[4,16,128]{2,1,0:T(8,128)S(1)} all-to-all(f32[4,16,128]{2,1,0:T(8,128)} %bitcast.63), channel_id=1, replica_groups=mesh['zh'=4,'z1'=2,'z0'=2,'xl'=2,'xh'=2,'y'=4,'core'=2] {'z0','xl'}, dimensions={0} | all-to-all | bytes 65536 | tf_op jit(solution)/shard_map/all_to_all | solution.py:148
  12.6 22.3 %all_to_all.61 = bf16[8,4,16,128]{3,2,1,0:T(8,128)(2,1)S(1)} all-to-all(bf16[8,4,16,128]{3,2,1,0:T(8,128)(2,1)S(1)} %broadcast_in_dim.13), channel_id=1, replica_groups=mesh['zh'=4,'z1'=2,'z0'=2,'xl'=2,'xh'=2,'y'=4,'core'=2] {'z1','zh'}, dimensions={0} | all-to-all | bytes 262144 | tf_op jit(solution)/shard_map/all_to_all | solution.py:148
  34.9 1.0 deal.3
  35.9 10.8 %all-to-all-start.2 = ((bf16[64,3,16,128]{3,2,1,0:T(8,128)(2,1)}), bf16[64,3,16,128]{3,2,1,0:T(8,128)(2,1)S(1)}, u32[]{:S(2)}, u32[]{:S(2)}) async-start(bf16[64,3,16,128]{3,2,1,0:T(8,128)(2,1)} %bitcast.5), calls=%async_computation.2 | async-start | bytes 1572864 | tf_op jit(solution)/shard_map/all_to_all | solution.py:148
  47.3 0.7 broadcast_select_fusion.1
  48.1 0.7 broadcast_select_fusion
  48.7 0.8 pad_add_fusion.index
  49.5 11.3 %all-to-all-done.2 = bf16[64,3,16,128]{3,2,1,0:T(8,128)(2,1)S(1)} async-done(((bf16[64,3,16,128]{3,2,1,0:T(8,128)(2,1)}), bf16[64,3,16,128]{3,2,1,0:T(8,128)(2,1)S(1)}, u32[]{:S(2)}, u32[]{:S(2)}) %all-to-all-start.2) | async-done | bytes 786464 | tf_op jit(solution)/shard_map/all_to_all | solution.py:148
  60.9 7.9 %terms.3 = bf16[4,16,3,16,128]{4,3,2,1,0:T(8,128)(2,1)} custom-call(s32[608]{0:T(1024)S(1)} %pad_add_fusion.index, bf16[4,16,3,16,128]{4,3,2,1,0:T(8,128)(2,1)S(1)} %bitcast.47, bf16[152,128,128]{2,1,0:T(8,128)(2,1)} %bitcast.57), custom_call_target="tpu_custom_call" | custom-call | tf_op jit(solution)/shard_map/terms/pallas_call | solution.py:80
  68.7 5.5 %all-to-all-start.3 = ((bf16[64,3,16,128]{3,2,1,0:T(8,128)(2,1)}), bf16[64,3,16,128]{3,2,1,0:T(8,128)(2,1)S(1)}, u32[]{:S(2)}, u32[]{:S(2)}) async-start(bf16[64,3,16,128]{3,2,1,0:T(8,128)(2,1)} %bitcast.8), calls=%async_computation.3 | async-start | bytes 1572864 | tf_op jit(solution)/shard_map/all_to_all | solution.py:148
  74.3 0.8 and_reduce_fusion
  75.1 13.4 %all-to-all-done.3 = bf16[64,3,16,128]{3,2,1,0:T(8,128)(2,1)S(1)} async-done(((bf16[64,3,16,128]{3,2,1,0:T(8,128)(2,1)}), bf16[64,3,16,128]{3,2,1,0:T(8,128)(2,1)S(1)}, u32[]{:S(2)}, u32[]{:S(2)}) %all-to-all-start.3) | async-done | bytes 786464 | tf_op jit(solution)/shard_map/all_to_all | solution.py:148
  88.5 0.8 merge.3
  89.2 3.4 %all-to-all-start.4 = ((bf16[2,4,4,16,128]{4,3,2,1,0:T(8,128)(2,1)}), bf16[2,4,4,16,128]{4,3,2,1,0:T(8,128)(2,1)S(1)}, u32[]{:S(2)}, u32[]{:S(2)}) async-start(bf16[2,4,4,16,128]{4,3,2,1,0:T(8,128)(2,1)} %merge.3), calls=%async_computation.4 | async-start | bytes 262144 | tf_op jit(solution)/shard_map/all_to_all | solution.py:148
  92.6 0.6 fusion.1
  93.3 5.7 %all-to-all-done.4 = bf16[2,4,4,16,128]{4,3,2,1,0:T(8,128)(2,1)S(1)} async-done(((bf16[2,4,4,16,128]{4,3,2,1,0:T(8,128)(2,1)}), bf16[2,4,4,16,128]{4,3,2,1,0:T(8,128)(2,1)S(1)}, u32[]{:S(2)}, u32[]{:S(2)}) %all-to-all-start.4) | async-done | bytes 131104 | tf_op jit(solution)/shard_map/all_to_all | solution.py:148
  99.1 19.7 %all-gather = bf16[16,4,16,128]{3,2,1,0:T(8,128)(2,1)S(1)} all-gather(bf16[4,4,16,128]{3,2,1,0:T(8,128)(2,1)S(1)} %reduce_sum.51), channel_id=2, replica_groups=mesh['zh'=4,'z1'=2,'z0'=2,'xl'=2,'xh'=2,'y'=4,'core'=2] {'zh'}, dimensions={0}, use_global_device_ids=true | all-gather | bytes 327680 | tf_op jit(solution)/shard_map/all_gather | solution.py:179
  118.8 5.8 %all-gather.1 = bf16[8,4,16,128]{3,2,1,0:T(8,128)(2,1)S(1)} all-gather(bf16[4,4,16,128]{3,2,1,0:T(8,128)(2,1)S(1)} %get-tuple-element.19), channel_id=3, replica_groups=mesh['zh'=4,'z1'=2,'z0'=2,'xl'=2,'xh'=2,'y'=4,'core'=2] {'z1'}, dimensions={0}, use_global_device_ids=true | all-gather | bytes 196608 | tf_op jit(solution)/shard_map/all_gather | solution.py:184
  124.8 19.7 %all_to_all.62 = bf16[64,3,16,128]{3,2,1,0:T(8,128)(2,1)S(1)} all-to-all(bf16[64,3,16,128]{3,2,1,0:T(8,128)(2,1)S(1)} %bitcast.43), channel_id=1, replica_groups=mesh['zh'=4,'z1'=2,'z0'=2,'xl'=2,'xh'=2,'y'=4,'core'=2] {'z0','xl','xh',..., dimensions={0} | all-to-all | bytes 1572864 | tf_op jit(solution)/shard_map/all_to_all | solution.py:148
  144.5 7.0 %terms.4 = bf16[4,16,3,16,128]{4,3,2,1,0:T(8,128)(2,1)S(1)} custom-call(s32[608]{0:T(1024)S(1)} %pad_add_fusion.index, bf16[4,16,3,16,128]{4,3,2,1,0:T(8,128)(2,1)S(1)} %bitcast.50, bf16[152,128,128]{2,1,0:T(8,128)(2,1)} %bitcast.58), custom_call_target="tpu_custom_call" | custom-call | tf_op jit(solution)/shard_map/terms/pallas_call | solution.py:80
  151.5 19.5 %all_to_all.63 = bf16[64,3,16,128]{3,2,1,0:T(8,128)(2,1)S(1)} all-to-all(bf16[64,3,16,128]{3,2,1,0:T(8,128)(2,1)S(1)} %bitcast.51), channel_id=1, replica_groups=mesh['zh'=4,'z1'=2,'z0'=2,'xl'=2,'xh'=2,'y'=4,'core'=2] {'z0','xl','xh',..., dimensions={0} | all-to-all | bytes 1572864 | tf_op jit(solution)/shard_map/all_to_all | solution.py:148
  171.0 0.1 merge.4
  171.1 8.8 %all_to_all.64 = bf16[2,4,4,16,128]{4,3,2,1,0:T(8,128)(2,1)S(1)} all-to-all(bf16[2,4,4,16,128]{4,3,2,1,0:T(8,128)(2,1)S(1)} %merge.4), channel_id=1, replica_groups=mesh['zh'=4,'z1'=2,'z0'=2,'xl'=2,'xh'=2,'y'=4,'core'=2] {'z1'}, dimensions={0} | all-to-all | bytes 262144 | tf_op jit(solution)/shard_map/all_to_all | solution.py:148
  180.0 19.2 %all-gather.2 = bf16[16,4,16,128]{3,2,1,0:T(8,128)(2,1)S(1)} all-gather(bf16[4,4,16,128]{3,2,1,0:T(8,128)(2,1)S(1)} %reduce_sum.53), channel_id=4, replica_groups=mesh['zh'=4,'z1'=2,'z0'=2,'xl'=2,'xh'=2,'y'=4,'core'=2] {'zh'}, dimensions={0}, use_global_device_ids=true | all-gather | bytes 327680 | tf_op jit(solution)/shard_map/all_gather | solution.py:179
  199.2 6.0 %all-gather.3 = bf16[8,4,16,128]{3,2,1,0:T(8,128)(2,1)S(1)} all-gather(bf16[4,4,16,128]{3,2,1,0:T(8,128)(2,1)S(1)} %get-tuple-element.17), channel_id=5, replica_groups=mesh['zh'=4,'z1'=2,'z0'=2,'xl'=2,'xh'=2,'y'=4,'core'=2] {'z1'}, dimensions={0}, use_global_device_ids=true | all-gather | bytes 196608 | tf_op jit(solution)/shard_map/all_gather | solution.py:184
  205.3 19.8 %all_to_all.65 = bf16[64,3,16,128]{3,2,1,0:T(8,128)(2,1)S(1)} all-to-all(bf16[64,3,16,128]{3,2,1,0:T(8,128)(2,1)S(1)} %bitcast.45), channel_id=1, replica_groups=mesh['zh'=4,'z1'=2,'z0'=2,'xl'=2,'xh'=2,'y'=4,'core'=2] {'z0','xl','xh',..., dimensions={0} | all-to-all | bytes 1572864 | tf_op jit(solution)/shard_map/all_to_all | solution.py:148
  225.1 7.0 %terms.5 = bf16[4,16,3,16,128]{4,3,2,1,0:T(8,128)(2,1)S(1)} custom-call(s32[608]{0:T(1024)S(1)} %pad_add_fusion.index, bf16[4,16,3,16,128]{4,3,2,1,0:T(8,128)(2,1)S(1)} %bitcast.48, bf16[152,128,128]{2,1,0:T(8,128)(2,1)} %bitcast.59), custom_call_target="tpu_custom_call" | custom-call | tf_op jit(solution)/shard_map/terms/pallas_call | solution.py:80
  232.1 19.5 %all_to_all.66 = bf16[64,3,16,128]{3,2,1,0:T(8,128)(2,1)S(1)} all-to-all(bf16[64,3,16,128]{3,2,1,0:T(8,128)(2,1)S(1)} %bitcast.49), channel_id=1, replica_groups=mesh['zh'=4,'z1'=2,'z0'=2,'xl'=2,'xh'=2,'y'=4,'core'=2] {'z0','xl','xh',..., dimensions={0} | all-to-all | bytes 1572864 | tf_op jit(solution)/shard_map/all_to_all | solution.py:148
  251.6 0.1 merge.5
  251.7 20.3 %all_to_all.67 = bf16[8,4,16,128]{3,2,1,0:T(8,128)(2,1)S(1)} all-to-all(bf16[8,4,16,128]{3,2,1,0:T(8,128)(2,1)S(1)} %bitcast.56), channel_id=1, replica_groups=mesh['zh'=4,'z1'=2,'z0'=2,'xl'=2,'xh'=2,'y'=4,'core'=2] {'z1','zh'}, dimensions={0} | all-to-all | bytes 262144 | tf_op jit(solution)/shard_map/all_to_all | solution.py:148
  272.0 8.1 %all_to_all.68 = f32[4,16,128]{2,1,0:T(8,128)S(1)} all-to-all(f32[4,16,128]{2,1,0:T(8,128)S(1)} %bitcast_subtract_fusion), channel_id=1, replica_groups=mesh['zh'=4,'z1'=2,'z0'=2,'xl'=2,'xh'=2,'y'=4,'core'=2] {'z0','xl'}, dimensions={0} | all-to-all | bytes 65536 | tf_op jit(solution)/shard_map/all_to_all | solution.py:148
  280.1 0.6 copy.9
  (15 shorter events, 0.5 us)
Async XLA Ops:
  35.9 38.4 %copy-start = (s32[4]{0:T(128)S(1)}, s32[4]{0:T(128)}, u32[]{:S(2)}) copy-start(s32[4]{0:T(128)} %constant.101.clone.1) | copy-start | bytes 52
  35.9 25.0 %all-to-all-start.2 = ((bf16[64,3,16,128]{3,2,1,0:T(8,128)(2,1)}), bf16[64,3,16,128]{3,2,1,0:T(8,128)(2,1)S(1)}, u32[]{:S(2)}, u32[]{:S(2)}) async-start(bf16[64,3,16,128]{3,2,1,0:T(8,128)(2,1)} %bitcast.5), calls=%async_computation.2 | async-start | bytes 1572864 | tf_op jit(solution)/shard_map/all_to_all | solution.py:148
  68.7 19.7 %all-to-all-start.3 = ((bf16[64,3,16,128]{3,2,1,0:T(8,128)(2,1)}), bf16[64,3,16,128]{3,2,1,0:T(8,128)(2,1)S(1)}, u32[]{:S(2)}, u32[]{:S(2)}) async-start(bf16[64,3,16,128]{3,2,1,0:T(8,128)(2,1)} %bitcast.8), calls=%async_computation.3 | async-start | bytes 1572864 | tf_op jit(solution)/shard_map/all_to_all | solution.py:148
  89.2 9.8 %all-to-all-start.4 = ((bf16[2,4,4,16,128]{4,3,2,1,0:T(8,128)(2,1)}), bf16[2,4,4,16,128]{4,3,2,1,0:T(8,128)(2,1)S(1)}, u32[]{:S(2)}, u32[]{:S(2)}) async-start(bf16[2,4,4,16,128]{4,3,2,1,0:T(8,128)(2,1)} %merge.3), calls=%async_computation.4 | async-start | bytes 262144 | tf_op jit(solution)/shard_map/all_to_all | solution.py:148

commit v4 on v3

--- a/solution.py
+++ b/solution.py
@@ -1,3 +1,5 @@
+import functools
+
 import jax
 import jax.numpy as jnp
 from jax import lax
@@ -8,12 +10,12 @@
 CENTER = 0.25
 HALF_WIDTH = 2.0
 DEGREE = 3
-CHUNKS, AHEAD = 8, 2
+CHUNKS, AHEAD = 4, 2
 QUAD = ("z0", "xl")
 ROW = ("zh", "z1") + QUAD
 COL = ("xh", "y", "core")
 UNIT = QUAD + COL
-UNITS = ("z1", "zh")
+SLABS = ("z1", "zh") + QUAD
 ALL = ROW + COL
 N_ZH, N_Z1, N_Q, N_COL = 4, 2, 4, 16
 N_HALF = N_ZH * N_Z1 * N_Q // N_COL
@@ -31,8 +33,12 @@
             yield h, b, rest // N_Q, zh, rest % N_Q
 
 
+def product(x, y, axis):
+    return lax.dot_general(x, y, (((1,), (axis,)), ((), ())), preferred_element_type=FLOAT)
+
+
 def terms_kernel(index, x_ref, blocks_hbm, out_ref, col_acc, row_acc, blocks, sems):
-    slots = blocks.shape[0]
+    slots, size = blocks.shape[:2]
     part = slots // CHUNKS
     width = x_ref.shape[0] * x_ref.shape[3]
     share = x_ref.shape[3]
@@ -54,16 +60,20 @@
         def _():
             copy(i + AHEAD).start()
 
-        for u in range(part):
-            s = base + u
-            block = blocks[s]
-            col = index[slots + s]
-            x_row = x_ref[:, index[s], N_HALF].reshape(width, block.shape[0])
-            x_col = x_ref[:, lax.rem(col, N_COL), lax.div(col, N_COL)].reshape(width, block.shape[0])
-            t = index[3 * slots + s]
-            col_acc[t] = col_acc[t] + lax.dot_general(x_row, block, (((1,), (0,)), ((), ())), preferred_element_type=FLOAT)
-            t = index[2 * slots + s]
-            row_acc[t] = row_acc[t] + lax.dot_general(x_col, block, (((1,), (1,)), ((), ())), preferred_element_type=FLOAT)
+        for s in range(0, part, 2):
+            pair = (base + s, base + s + 1)
+            both = [blocks[t] for t in pair]
+            x_row = [x_ref[:, index[t], N_HALF].reshape(width, size) for t in pair]
+            cols = [index[slots + t] for t in pair]
+            x_col = [x_ref[:, lax.rem(c, N_COL), lax.div(c, N_COL)].reshape(width, size) for c in cols]
+            by_col = product(jnp.concatenate(x_row), jnp.concatenate(both, axis=1), 0)
+            by_row = product(jnp.concatenate(x_col), jnp.concatenate(both), 1)
+            for i, t in enumerate(pair):
+                own = (slice(i * width, (i + 1) * width), slice(i * size, (i + 1) * size))
+                to = index[3 * slots + t]
+                col_acc[to] = col_acc[to] + by_col[own]
+                to = index[2 * slots + t]
+                row_acc[to] = row_acc[to] + by_row[own]
         return carry
 
     lax.fori_loop(0, CHUNKS, chunk, 0)
@@ -93,7 +103,7 @@
     )(index, x, blocks)
 
 
-def merge_kernel(got_ref, out_ref, acc):
+def merge_kernel(extra_ref, got_ref, out_ref, acc):
     for h, b, z1, zh, q in places():
         piece = got_ref[0, b, h].astype(FLOAT)
         for k in range(1, N_Q):
@@ -105,20 +115,23 @@
         for b in range(1, N_COL):
             piece = piece + got_ref[q, b, N_HALF].astype(FLOAT)
         acc[z1, zh, q] = acc[z1, zh, q] + piece
+    if extra_ref is not None:
+        acc[z1, zh] = acc[z1, zh] + extra_ref[...]
     out_ref[...] = acc[...].astype(WIRE)
 
 
-def merge(got):
+def merge(got, extra):
     shape = (N_Z1, N_ZH, N_Q) + got.shape[3:]
+    given = [got] if extra is None else [extra, got]
     return pl.pallas_call(
-        merge_kernel,
+        functools.partial(merge_kernel, None) if extra is None else merge_kernel,
         out_shape=jax.ShapeDtypeStruct(shape, WIRE),
-        in_specs=[VMEM],
+        in_specs=[VMEM] * len(given),
         out_specs=VMEM,
         scratch_shapes=[pltpu.VMEM(shape, FLOAT)],
         compiler_params=pltpu.CompilerParams(vmem_limit_bytes=SMALL),
         name="merge",
-    )(got)
+    )(*given)
 
 
 def deal_kernel(all_ref, out_ref):
@@ -165,15 +178,15 @@
     live = (jnp.arange(slots, dtype=jnp.int32) < counts[0, 0]) & (global_rows <= global_cols)
     index = jnp.concatenate([rows, cols, jnp.where(live, rows, N_COL), jnp.where(live, cols, N_HALF * N_COL)])
 
-    def unit_sums(pieces):
+    def unit_sums(pieces, extra=None):
         got = exchange(deal(pieces).reshape(N_Q * N_COL, N_HALF + 1, *pieces.shape[3:]), UNIT)
         out = terms(got.reshape(N_Q, N_COL, *got.shape[1:]), blocks, index)
-        return merge(exchange(out.reshape(got.shape), UNIT).reshape(out.shape))
-
-    quarter = exchange(vectors.reshape(N_Q, width // N_Q, size), QUAD)
-    copies = jnp.broadcast_to(quarter.astype(WIRE)[None], (N_Z1 * N_ZH,) + quarter.shape)
-    wire = exchange(copies, UNITS).reshape(N_Z1, N_ZH, *quarter.shape)
-    before, now = None, wire[z1].astype(FLOAT).at[zh].set(quarter)
+        return merge(exchange(out.reshape(got.shape), UNIT).reshape(out.shape), extra)
+
+    quarters = vectors.astype(WIRE).reshape(1, N_Q, width // N_Q, size)
+    copies = jnp.broadcast_to(quarters, (N_Z1 * N_ZH,) + quarters.shape[1:]).reshape(-1, *quarters.shape[2:])
+    wire = exchange(copies, SLABS).reshape(N_Z1, N_ZH, *quarters.shape[1:])
+    before, now = None, wire[z1].astype(FLOAT)
     for step in range(DEGREE - 1):
         pair_sums = total(exchange(unit_sums(wire), "z1")).astype(WIRE)
         image = total(lax.all_gather(pair_sums, "zh"))
@@ -182,10 +195,9 @@
             after = 2.0 * (image - CENTER * now) / HALF_WIDTH - before
         before, now = now, after
         wire = lax.all_gather(now.astype(WIRE), "z1")
-    sums = unit_sums(wire)
-    image = total(exchange(sums.reshape(-1, *sums.shape[2:]), UNITS))
-    own = 2.0 * (image - CENTER * now[zh]) / HALF_WIDTH - before[zh]
-    return exchange(own, QUAD).reshape(width, size)
+    sums = unit_sums(wire, -(CENTER * now[zh] + HALF_WIDTH / 2.0 * before[zh]))
+    got = exchange(sums.reshape(-1, *sums.shape[3:]), SLABS).reshape(N_Z1 * N_ZH, *quarters.shape[1:])
+    return (2.0 * total(got) / HALF_WIDTH).reshape(width, size)
 
 
 def solution(mesh):

time: 282 us -> 266 us (0.943)
  the two profiles are of different devices: /device:TPU:2 before, /device:TPU:32 now
where the time goes in v4:
time: 266 us
  blocking collectives  194 us (73%)
  waiting for transfers between devices  30 us (11%)
  Pallas kernels  18.9 us (7%)
  starting transfers between devices  18.1 us (7%)
  other arithmetic  3.82 us (1%)
    all_to_all x7, blocking collectives, exchange(): return lax.all_to_all(x, axes, 0, 0, tiled=True)  142 us
    all_gather x2, blocking collectives, local(): image = total(lax.all_gather(pair_sums, 'zh'))  40.1 us
    all_to_all x3, waiting for transfers between devices, exchange(): return lax.all_to_all(x, axes, 0, 0, tiled=True)  30 us
    all_to_all x3, starting transfers between devices, exchange(): return lax.all_to_all(x, axes, 0, 0, tiled=True)  18.1 us
    pallas_call x3, Pallas kernels, terms(): pl.pallas_call(terms_kernel, out_shape=jax.ShapeDtypeStruct(x.shape, WIRE...  16.7 us
    all_gather x2, blocking collectives, local(): wire = lax.all_gather(now.astype(WIRE), 'z1')  11.7 us
  transfers between devices with their start and end apart: 3, of which 3 were waited for; matrix products, arithmetic and copies ran while one was open for 1% of the time, Pallas kernels for 0%

profile of v4, /device:TPU:32, one launch (start us, length us, event | category | flops | bytes accessed | tf_op | source)
XLA Modules:
  0.0 265.7 jit_solution(5349923524733364094)
XLA Ops:
  0.0 0.8 convert_element_type.37
  0.8 31.1 %all_to_all.50 = bf16[32,16,128]{2,1,0:T(8,128)(2,1)S(1)} all-to-all(bf16[32,16,128]{2,1,0:T(8,128)(2,1)S(1)} %bitcast.66), channel_id=1, replica_groups=mesh['zh'=4,'z1'=2,'z0'=2,'xl'=2,'xh'=2,'y'=4,'core'=2] {'z1','zh','z0',..., dimensions={0} | all-to-all | bytes 262144 | tf_op jit(solution)/shard_map/all_to_all | solution.py:161
  31.8 1.0 deal.3
  32.8 8.8 %all-to-all-start.1 = ((bf16[64,3,16,128]{3,2,1,0:T(8,128)(2,1)}), bf16[64,3,16,128]{3,2,1,0:T(8,128)(2,1)S(1)}, u32[]{:S(2)}, u32[]{:S(2)}) async-start(bf16[64,3,16,128]{3,2,1,0:T(8,128)(2,1)} %bitcast.6), calls=%async_computation.1 | async-start | bytes 1572864 | tf_op jit(solution)/shard_map/all_to_all | solution.py:161
  42.3 0.7 broadcast_select_fusion.1
  43.0 0.7 broadcast_select_fusion
  43.7 0.8 pad_add_fusion.index
  44.4 11.0 %all-to-all-done.1 = bf16[64,3,16,128]{3,2,1,0:T(8,128)(2,1)S(1)} async-done(((bf16[64,3,16,128]{3,2,1,0:T(8,128)(2,1)}), bf16[64,3,16,128]{3,2,1,0:T(8,128)(2,1)S(1)}, u32[]{:S(2)}, u32[]{:S(2)}) %all-to-all-start.1) | async-done | bytes 786464 | tf_op jit(solution)/shard_map/all_to_all | solution.py:161
  55.4 5.3 %terms.3 = bf16[4,16,3,16,128]{4,3,2,1,0:T(8,128)(2,1)S(1)} custom-call(s32[608]{0:T(1024)S(1)} %pad_add_fusion.index, bf16[4,16,3,16,128]{4,3,2,1,0:T(8,128)(2,1)S(1)} %bitcast.49, bf16[152,128,128]{2,1,0:T(8,128)(2,1)} %bitcast.60), custom_call_target="tpu_custom_call" | custom-call | tf_op jit(solution)/shard_map/terms/pallas_call | solution.py:90
  60.7 19.6 %all_to_all.51 = bf16[64,3,16,128]{3,2,1,0:T(8,128)(2,1)S(1)} all-to-all(bf16[64,3,16,128]{3,2,1,0:T(8,128)(2,1)S(1)} %bitcast.51), channel_id=1, replica_groups=mesh['zh'=4,'z1'=2,'z0'=2,'xl'=2,'xh'=2,'y'=4,'core'=2] {'z0','xl','xh',..., dimensions={0} | all-to-all | bytes 1572864 | tf_op jit(solution)/shard_map/all_to_all | solution.py:161
  80.2 0.8 merge.3
  81.0 3.4 %all-to-all-start.3 = ((bf16[2,4,4,16,128]{4,3,2,1,0:T(8,128)(2,1)}), bf16[2,4,4,16,128]{4,3,2,1,0:T(8,128)(2,1)S(1)}, u32[]{:S(2)}, u32[]{:S(2)}) async-start(bf16[2,4,4,16,128]{4,3,2,1,0:T(8,128)(2,1)} %merge.3), calls=%async_computation.3 | async-start | bytes 262144 | tf_op jit(solution)/shard_map/all_to_all | solution.py:161
  84.4 5.4 %all-to-all-done.3 = bf16[2,4,4,16,128]{4,3,2,1,0:T(8,128)(2,1)S(1)} async-done(((bf16[2,4,4,16,128]{4,3,2,1,0:T(8,128)(2,1)}), bf16[2,4,4,16,128]{4,3,2,1,0:T(8,128)(2,1)S(1)}, u32[]{:S(2)}, u32[]{:S(2)}) %all-to-all-start.3) | async-done | bytes 131104 | tf_op jit(solution)/shard_map/all_to_all | solution.py:161
  89.8 19.7 %all-gather = bf16[16,4,16,128]{3,2,1,0:T(8,128)(2,1)S(1)} all-gather(bf16[4,4,16,128]{3,2,1,0:T(8,128)(2,1)S(1)} %reduce_sum.57), channel_id=2, replica_groups=mesh['zh'=4,'z1'=2,'z0'=2,'xl'=2,'xh'=2,'y'=4,'core'=2] {'zh'}, dimensions={0}, use_global_device_ids=true | all-gather | bytes 327680 | tf_op jit(solution)/shard_map/all_gather | solution.py:192
  109.6 5.9 %all_gather.22.all_ref = bf16[2,4,4,16,128]{4,3,2,1,0:T(8,128)(2,1)S(1)} all-gather(bf16[1,4,4,16,128]{4,3,2,1,0:T(8,128)(2,1)S(1)} %multiply_convert_fusion), channel_id=1, replica_groups=mesh['zh'=4,'z1'=2,'z0'=2,'xl'=2,'xh'=2,'y'=4,'core'=2] {'z1'}, dimensions={0}, use_global_device_ids=true | all-gather | bytes 196608 | tf_op jit(solution)/shard_map/all_gather | solution.py:197
  115.4 0.1 deal.4
  115.5 20.7 %all_to_all.52 = bf16[64,3,16,128]{3,2,1,0:T(8,128)(2,1)S(1)} all-to-all(bf16[64,3,16,128]{3,2,1,0:T(8,128)(2,1)S(1)} %bitcast.45), channel_id=1, replica_groups=mesh['zh'=4,'z1'=2,'z0'=2,'xl'=2,'xh'=2,'y'=4,'core'=2] {'z0','xl','xh',..., dimensions={0} | all-to-all | bytes 1572864 | tf_op jit(solution)/shard_map/all_to_all | solution.py:161
  136.3 5.3 %terms.4 = bf16[4,16,3,16,128]{4,3,2,1,0:T(8,128)(2,1)S(1)} custom-call(s32[608]{0:T(1024)S(1)} %pad_add_fusion.index, bf16[4,16,3,16,128]{4,3,2,1,0:T(8,128)(2,1)S(1)} %bitcast.52, bf16[152,128,128]{2,1,0:T(8,128)(2,1)} %bitcast.61), custom_call_target="tpu_custom_call" | custom-call | tf_op jit(solution)/shard_map/terms/pallas_call | solution.py:90
  141.5 19.5 %all_to_all.53 = bf16[64,3,16,128]{3,2,1,0:T(8,128)(2,1)S(1)} all-to-all(bf16[64,3,16,128]{3,2,1,0:T(8,128)(2,1)S(1)} %bitcast.53), channel_id=1, replica_groups=mesh['zh'=4,'z1'=2,'z0'=2,'xl'=2,'xh'=2,'y'=4,'core'=2] {'z0','xl','xh',..., dimensions={0} | all-to-all | bytes 1572864 | tf_op jit(solution)/shard_map/all_to_all | solution.py:161
  161.1 0.1 merge.4
  161.2 7.7 %all_to_all.54 = bf16[2,4,4,16,128]{4,3,2,1,0:T(8,128)(2,1)S(1)} all-to-all(bf16[2,4,4,16,128]{4,3,2,1,0:T(8,128)(2,1)S(1)} %merge.4), channel_id=1, replica_groups=mesh['zh'=4,'z1'=2,'z0'=2,'xl'=2,'xh'=2,'y'=4,'core'=2] {'z1'}, dimensions={0} | all-to-all | bytes 262144 | tf_op jit(solution)/shard_map/all_to_all | solution.py:161
  169.0 20.3 %all-gather.1 = bf16[16,4,16,128]{3,2,1,0:T(8,128)(2,1)S(1)} all-gather(bf16[4,4,16,128]{3,2,1,0:T(8,128)(2,1)S(1)} %reduce_sum.60), channel_id=3, replica_groups=mesh['zh'=4,'z1'=2,'z0'=2,'xl'=2,'xh'=2,'y'=4,'core'=2] {'zh'}, dimensions={0}, use_global_device_ids=true | all-gather | bytes 327680 | tf_op jit(solution)/shard_map/all_gather | solution.py:192
  189.4 5.8 %all_gather.25.all_ref = bf16[2,4,4,16,128]{4,3,2,1,0:T(8,128)(2,1)S(1)} all-gather(bf16[1,4,4,16,128]{4,3,2,1,0:T(8,128)(2,1)S(1)} %fusion.1), channel_id=1, replica_groups=mesh['zh'=4,'z1'=2,'z0'=2,'xl'=2,'xh'=2,'y'=4,'core'=2] {'z1'}, dimensions={0}, use_global_device_ids=true | all-gather | bytes 196608 | tf_op jit(solution)/shard_map/all_gather | solution.py:197
  195.2 0.1 deal.5
  195.3 19.9 %all_to_all.55 = bf16[64,3,16,128]{3,2,1,0:T(8,128)(2,1)S(1)} all-to-all(bf16[64,3,16,128]{3,2,1,0:T(8,128)(2,1)S(1)} %bitcast.47), channel_id=1, replica_groups=mesh['zh'=4,'z1'=2,'z0'=2,'xl'=2,'xh'=2,'y'=4,'core'=2] {'z0','xl','xh',..., dimensions={0} | all-to-all | bytes 1572864 | tf_op jit(solution)/shard_map/all_to_all | solution.py:161
  215.2 6.1 %terms.5 = bf16[4,16,3,16,128]{4,3,2,1,0:T(8,128)(2,1)} custom-call(s32[608]{0:T(1024)S(1)} %pad_add_fusion.index, bf16[4,16,3,16,128]{4,3,2,1,0:T(8,128)(2,1)S(1)} %bitcast.50, bf16[152,128,128]{2,1,0:T(8,128)(2,1)} %bitcast.62), custom_call_target="tpu_custom_call" | custom-call | tf_op jit(solution)/shard_map/terms/pallas_call | solution.py:90
  221.4 6.0 %all-to-all-start.8 = ((bf16[64,3,16,128]{3,2,1,0:T(8,128)(2,1)}), bf16[64,3,16,128]{3,2,1,0:T(8,128)(2,1)S(1)}, u32[]{:S(2)}, u32[]{:S(2)}) async-start(bf16[64,3,16,128]{3,2,1,0:T(8,128)(2,1)} %bitcast.23), calls=%async_computation.8 | async-start | bytes 1572864 | tf_op jit(solution)/shard_map/all_to_all | solution.py:161
  227.4 13.7 %all-to-all-done.8 = bf16[64,3,16,128]{3,2,1,0:T(8,128)(2,1)S(1)} async-done(((bf16[64,3,16,128]{3,2,1,0:T(8,128)(2,1)}), bf16[64,3,16,128]{3,2,1,0:T(8,128)(2,1)S(1)}, u32[]{:S(2)}, u32[]{:S(2)}) %all-to-all-start.8) | async-done | bytes 786464 | tf_op jit(solution)/shard_map/all_to_all | solution.py:161
  241.1 0.1 merge.5
  241.3 23.7 %all_to_all.56 = bf16[32,16,128]{2,1,0:T(8,128)(2,1)S(1)} all-to-all(bf16[32,16,128]{2,1,0:T(8,128)(2,1)S(1)} %bitcast.59), channel_id=1, replica_groups=mesh['zh'=4,'z1'=2,'z0'=2,'xl'=2,'xh'=2,'y'=4,'core'=2] {'z1','zh','z0',..., dimensions={0} | all-to-all | bytes 262144 | tf_op jit(solution)/shard_map/all_to_all | solution.py:161
  265.0 0.6 convert_reduce_fusion.2
  (10 shorter events, 0.3 us)
Async XLA Ops:
  32.8 22.6 %all-to-all-start.1 = ((bf16[64,3,16,128]{3,2,1,0:T(8,128)(2,1)}), bf16[64,3,16,128]{3,2,1,0:T(8,128)(2,1)S(1)}, u32[]{:S(2)}, u32[]{:S(2)}) async-start(bf16[64,3,16,128]{3,2,1,0:T(8,128)(2,1)} %bitcast.6), calls=%async_computation.1 | async-start | bytes 1572864 | tf_op jit(solution)/shard_map/all_to_all | solution.py:161
  81.0 8.7 %all-to-all-start.3 = ((bf16[2,4,4,16,128]{4,3,2,1,0:T(8,128)(2,1)}), bf16[2,4,4,16,128]{4,3,2,1,0:T(8,128)(2,1)S(1)}, u32[]{:S(2)}, u32[]{:S(2)}) async-start(bf16[2,4,4,16,128]{4,3,2,1,0:T(8,128)(2,1)} %merge.3), calls=%async_computation.3 | async-start | bytes 262144 | tf_op jit(solution)/shard_map/all_to_all | solution.py:161
  221.4 19.8 %all-to-all-start.8 = ((bf16[64,3,16,128]{3,2,1,0:T(8,128)(2,1)}), bf16[64,3,16,128]{3,2,1,0:T(8,128)(2,1)S(1)}, u32[]{:S(2)}, u32[]{:S(2)}) async-start(bf16[64,3,16,128]{3,2,1,0:T(8,128)(2,1)} %bitcast.23), calls=%async_computation.8 | async-start | bytes 1572864 | tf_op jit(solution)/shard_map/all_to_all | solution.py:161

commit v5 on v4

--- a/solution.py
+++ b/solution.py
@@ -103,7 +103,8 @@
     )(index, x, blocks)
 
 
-def merge_kernel(extra_ref, got_ref, out_ref, acc):
+def merge_kernel(last, got_ref, *refs):
+    acc = refs[-1]
     for h, b, z1, zh, q in places():
         piece = got_ref[0, b, h].astype(FLOAT)
         for k in range(1, N_Q):
@@ -115,23 +116,29 @@
         for b in range(1, N_COL):
             piece = piece + got_ref[q, b, N_HALF].astype(FLOAT)
         acc[z1, zh, q] = acc[z1, zh, q] + piece
-    if extra_ref is not None:
+    if last:
+        extra_ref, out_ref = refs[:2]
         acc[z1, zh] = acc[z1, zh] + extra_ref[...]
-    out_ref[...] = acc[...].astype(WIRE)
+        out_ref[...] = acc[...].astype(WIRE)
+    else:
+        kept_ref, sent_ref = refs[:2]
+        kept_ref[...] = acc[z1]
+        sent_ref[...] = acc[1 - z1].astype(WIRE)
 
 
 def merge(got, extra):
     shape = (N_Z1, N_ZH, N_Q) + got.shape[3:]
-    given = [got] if extra is None else [extra, got]
+    last = extra is not None
+    kept, sent = jax.ShapeDtypeStruct(shape[1:], FLOAT), jax.ShapeDtypeStruct(shape[1:], WIRE)
     return pl.pallas_call(
-        functools.partial(merge_kernel, None) if extra is None else merge_kernel,
-        out_shape=jax.ShapeDtypeStruct(shape, WIRE),
-        in_specs=[VMEM] * len(given),
-        out_specs=VMEM,
+        functools.partial(merge_kernel, last),
+        out_shape=jax.ShapeDtypeStruct(shape, WIRE) if last else (kept, sent),
+        in_specs=[VMEM] * (2 if last else 1),
+        out_specs=VMEM if last else (VMEM, VMEM),
         scratch_shapes=[pltpu.VMEM(shape, FLOAT)],
         compiler_params=pltpu.CompilerParams(vmem_limit_bytes=SMALL),
         name="merge",
-    )(*given)
+    )(*((got, extra) if last else (got,)))
 
 
 def deal_kernel(all_ref, out_ref):
@@ -188,8 +195,9 @@
     wire = exchange(copies, SLABS).reshape(N_Z1, N_ZH, *quarters.shape[1:])
     before, now = None, wire[z1].astype(FLOAT)
     for step in range(DEGREE - 1):
-        pair_sums = total(exchange(unit_sums(wire), "z1")).astype(WIRE)
-        image = total(lax.all_gather(pair_sums, "zh"))
+        kept, sent = unit_sums(wire)
+        pair_sums = kept + lax.ppermute(sent, "z1", [(0, 1), (1, 0)]).astype(FLOAT)
+        image = total(lax.all_gather(pair_sums.astype(WIRE), "zh"))
         after = (image - CENTER * now) / HALF_WIDTH
         if step > 0:
             after = 2.0 * (image - CENTER * now) / HALF_WIDTH - before

time: 266 us -> 263 us (0.989)
  blocking collectives: 194 us -> 186 us
  starting transfers between devices: 18.1 us -> 21 us
    all_to_all x7 -> x6, blocking collectives: 142 us -> 134 us  [exchange(): return lax.all_to_all(x, axes, 0, 0, tiled=True)]
    ppermute x0 -> x2, waiting for transfers between devices: none -> 7.88 us  [local(): pair_sums = kept + lax.ppermute(sent, 'z1', [(0, 1), (1, 0)]).astype(FLOAT)]
    ppermute x0 -> x2, starting transfers between devices: none -> 6.22 us  [local(): pair_sums = kept + lax.ppermute(sent, 'z1', [(0, 1), (1, 0)]).astype(FLOAT)]
    all_to_all x3 -> x2, waiting for transfers between devices: 30 us -> 24.7 us  [exchange(): return lax.all_to_all(x, axes, 0, 0, tiled=True)]
    all_to_all x3 -> x2, starting transfers between devices: 18.1 us -> 14.7 us  [exchange(): return lax.all_to_all(x, axes, 0, 0, tiled=True)]
    all_gather x2, blocking collectives: 40.1 us -> 37.2 us  [local(): image = total(lax.all_gather(pair_sums.astype(WIRE), 'zh'))]
    all_gather x2, blocking collectives: 11.7 us -> 14.5 us  [local(): wire = lax.all_gather(now.astype(WIRE), 'z1')]
  transfers between devices with their start and end apart: 3 -> 4, of which waited for: 3 -> 4; matrix products, arithmetic and copies ran while one was open for 1% -> 1% of each run, Pallas kernels for 0% -> 0%
where the time goes in v5:
time: 263 us; the launch traced here: 262 us
  blocking collectives  186 us (71%)
  waiting for transfers between devices  32.5 us (12%)
  starting transfers between devices  21 us (8%)
  Pallas kernels  18.2 us (7%)
  other arithmetic  3.81 us (1%)
    all_to_all x6, blocking collectives, exchange(): return lax.all_to_all(x, axes, 0, 0, tiled=True)  134 us
    all_gather x2, blocking collectives, local(): image = total(lax.all_gather(pair_sums.astype(WIRE), 'zh'))  37.2 us
    all_to_all x2, waiting for transfers between devices, exchange(): return lax.all_to_all(x, axes, 0, 0, tiled=True)  24.7 us
    pallas_call x3, Pallas kernels, terms(): pl.pallas_call(terms_kernel, out_shape=jax.ShapeDtypeStruct(x.shape, WIRE...  16.7 us
    all_to_all x2, starting transfers between devices, exchange(): return lax.all_to_all(x, axes, 0, 0, tiled=True)  14.7 us
    all_gather x2, blocking collectives, local(): wire = lax.all_gather(now.astype(WIRE), 'z1')  14.5 us
    ppermute x2, waiting for transfers between devices, local(): pair_sums = kept + lax.ppermute(sent, 'z1', [(0, 1), (1, 0)]).astype(FLOAT)  7.88 us
    ppermute x2, starting transfers between devices, local(): pair_sums = kept + lax.ppermute(sent, 'z1', [(0, 1), (1, 0)]).astype(FLOAT)  6.22 us
  transfers between devices with their start and end apart: 4, of which 4 were waited for; matrix products, arithmetic and copies ran while one was open for 1% of the time, Pallas kernels for 0%

profile of v5, /device:TPU:32, one launch (start us, length us, event | category | flops | bytes accessed | tf_op | source)
XLA Modules:
  0.0 262.3 jit_solution(16563567835511177108)
XLA Ops:
  0.0 0.8 convert_element_type.45
  0.8 31.1 %all_to_all.40 = bf16[32,16,128]{2,1,0:T(8,128)(2,1)S(1)} all-to-all(bf16[32,16,128]{2,1,0:T(8,128)(2,1)S(1)} %bitcast.66), channel_id=1, replica_groups=mesh['zh'=4,'z1'=2,'z0'=2,'xl'=2,'xh'=2,'y'=4,'core'=2] {'z1','zh','z0',..., dimensions={0} | all-to-all | bytes 262144 | tf_op jit(solution)/shard_map/all_to_all | solution.py:168
  31.8 1.0 deal.3
  32.8 8.8 %all-to-all-start.1 = ((bf16[64,3,16,128]{3,2,1,0:T(8,128)(2,1)}), bf16[64,3,16,128]{3,2,1,0:T(8,128)(2,1)S(1)}, u32[]{:S(2)}, u32[]{:S(2)}) async-start(bf16[64,3,16,128]{3,2,1,0:T(8,128)(2,1)} %bitcast.6), calls=%async_computation.1 | async-start | bytes 1572864 | tf_op jit(solution)/shard_map/all_to_all | solution.py:168
  42.3 0.7 broadcast_select_fusion.1
  43.0 0.7 broadcast_select_fusion
  43.7 0.8 pad_add_fusion.index
  44.5 11.0 %all-to-all-done.1 = bf16[64,3,16,128]{3,2,1,0:T(8,128)(2,1)S(1)} async-done(((bf16[64,3,16,128]{3,2,1,0:T(8,128)(2,1)}), bf16[64,3,16,128]{3,2,1,0:T(8,128)(2,1)S(1)}, u32[]{:S(2)}, u32[]{:S(2)}) %all-to-all-start.1) | async-done | bytes 786464 | tf_op jit(solution)/shard_map/all_to_all | solution.py:168
  55.4 5.3 %terms.3 = bf16[4,16,3,16,128]{4,3,2,1,0:T(8,128)(2,1)S(1)} custom-call(s32[608]{0:T(1024)S(1)} %pad_add_fusion.index, bf16[4,16,3,16,128]{4,3,2,1,0:T(8,128)(2,1)S(1)} %bitcast.49, bf16[152,128,128]{2,1,0:T(8,128)(2,1)} %bitcast.60), custom_call_target="tpu_custom_call" | custom-call | tf_op jit(solution)/shard_map/terms/pallas_call | solution.py:90
  60.7 19.5 %all_to_all.41 = bf16[64,3,16,128]{3,2,1,0:T(8,128)(2,1)S(1)} all-to-all(bf16[64,3,16,128]{3,2,1,0:T(8,128)(2,1)S(1)} %bitcast.51), channel_id=1, replica_groups=mesh['zh'=4,'z1'=2,'z0'=2,'xl'=2,'xh'=2,'y'=4,'core'=2] {'z0','xl','xh',..., dimensions={0} | all-to-all | bytes 1572864 | tf_op jit(solution)/shard_map/all_to_all | solution.py:168
  80.2 0.1 merge.3
  80.4 3.0 %collective-permute-start = (bf16[4,4,16,128]{3,2,1,0:T(8,128)(2,1)S(1)}, bf16[4,4,16,128]{3,2,1,0:T(8,128)(2,1)S(1)}, u32[]{:S(2)}, u32[]{:S(2)}) collective-permute-start(bf16[4,4,16,128]{3,2,1,0:T(8,128)(2,1)S(1)} %get-tuple-element.10), channel_id=1, source_target_pairs={{0,64},{64,0},{1,65},{65,1},{2,66},{66,2},{3,67},{67,3},{4,68},{68... | collective-permute-start | bytes 196616 | tf_op jit(solution)/shard_map/ppermute | solution.py:199
  83.3 4.1 %collective-permute-done = bf16[4,4,16,128]{3,2,1,0:T(8,128)(2,1)S(1)} collective-permute-done((bf16[4,4,16,128]{3,2,1,0:T(8,128)(2,1)S(1)}, bf16[4,4,16,128]{3,2,1,0:T(8,128)(2,1)S(1)}, u32[]{:S(2)}, u32[]{:S(2)}) %collective-permute-start) | collective-permute-done | bytes 65568 | tf_op jit(solution)/shard_map/ppermute | solution.py:199
  87.4 18.4 %all-gather = bf16[16,4,16,128]{3,2,1,0:T(8,128)(2,1)S(1)} all-gather(bf16[4,4,16,128]{3,2,1,0:T(8,128)(2,1)S(1)} %add_convert_fusion.1), channel_id=2, replica_groups=mesh['zh'=4,'z1'=2,'z0'=2,'xl'=2,'xh'=2,'y'=4,'core'=2] {'zh'}, dimensions={0}, use_global_device_ids=true | all-gather | bytes 327680 | tf_op jit(solution)/shard_map/all_gather | solution.py:200
  105.9 7.3 %all_gather.22.all_ref = bf16[2,4,4,16,128]{4,3,2,1,0:T(8,128)(2,1)S(1)} all-gather(bf16[1,4,4,16,128]{4,3,2,1,0:T(8,128)(2,1)S(1)} %multiply_convert_fusion), channel_id=1, replica_groups=mesh['zh'=4,'z1'=2,'z0'=2,'xl'=2,'xh'=2,'y'=4,'core'=2] {'z1'}, dimensions={0}, use_global_device_ids=true | all-gather | bytes 196608 | tf_op jit(solution)/shard_map/all_gather | solution.py:205
  113.2 0.1 deal.4
  113.3 20.6 %all_to_all.42 = bf16[64,3,16,128]{3,2,1,0:T(8,128)(2,1)S(1)} all-to-all(bf16[64,3,16,128]{3,2,1,0:T(8,128)(2,1)S(1)} %bitcast.46), channel_id=1, replica_groups=mesh['zh'=4,'z1'=2,'z0'=2,'xl'=2,'xh'=2,'y'=4,'core'=2] {'z0','xl','xh',..., dimensions={0} | all-to-all | bytes 1572864 | tf_op jit(solution)/shard_map/all_to_all | solution.py:168
  133.9 5.2 %terms.4 = bf16[4,16,3,16,128]{4,3,2,1,0:T(8,128)(2,1)S(1)} custom-call(s32[608]{0:T(1024)S(1)} %pad_add_fusion.index, bf16[4,16,3,16,128]{4,3,2,1,0:T(8,128)(2,1)S(1)} %bitcast.52, bf16[152,128,128]{2,1,0:T(8,128)(2,1)} %bitcast.61), custom_call_target="tpu_custom_call" | custom-call | tf_op jit(solution)/shard_map/terms/pallas_call | solution.py:90
  139.2 19.5 %all_to_all.43 = bf16[64,3,16,128]{3,2,1,0:T(8,128)(2,1)S(1)} all-to-all(bf16[64,3,16,128]{3,2,1,0:T(8,128)(2,1)S(1)} %bitcast.53), channel_id=1, replica_groups=mesh['zh'=4,'z1'=2,'z0'=2,'xl'=2,'xh'=2,'y'=4,'core'=2] {'z0','xl','xh',..., dimensions={0} | all-to-all | bytes 1572864 | tf_op jit(solution)/shard_map/all_to_all | solution.py:168
  158.7 0.1 merge.4
  158.9 3.3 %collective-permute-start.1 = (bf16[4,4,16,128]{3,2,1,0:T(8,128)(2,1)S(1)}, bf16[4,4,16,128]{3,2,1,0:T(8,128)(2,1)S(1)}, u32[]{:S(2)}, u32[]{:S(2)}) collective-permute-start(bf16[4,4,16,128]{3,2,1,0:T(8,128)(2,1)S(1)} %get-tuple-element.12), channel_id=1, source_target_pairs={{0,64},{64,0},{1,65},{65,1},{2,66},{66,2},{3,67},{67,3},{4,68},{68... | collective-permute-start | bytes 196616 | tf_op jit(solution)/shard_map/ppermute | solution.py:199
  162.1 3.8 %collective-permute-done.1 = bf16[4,4,16,128]{3,2,1,0:T(8,128)(2,1)S(1)} collective-permute-done((bf16[4,4,16,128]{3,2,1,0:T(8,128)(2,1)S(1)}, bf16[4,4,16,128]{3,2,1,0:T(8,128)(2,1)S(1)}, u32[]{:S(2)}, u32[]{:S(2)}) %collective-permute-start.1) | collective-permute-done | bytes 65568 | tf_op jit(solution)/shard_map/ppermute | solution.py:199
  165.9 18.8 %all-gather.1 = bf16[16,4,16,128]{3,2,1,0:T(8,128)(2,1)S(1)} all-gather(bf16[4,4,16,128]{3,2,1,0:T(8,128)(2,1)S(1)} %add_convert_fusion), channel_id=3, replica_groups=mesh['zh'=4,'z1'=2,'z0'=2,'xl'=2,'xh'=2,'y'=4,'core'=2] {'zh'}, dimensions={0}, use_global_device_ids=true | all-gather | bytes 327680 | tf_op jit(solution)/shard_map/all_gather | solution.py:200
  184.8 7.2 %all_gather.25.all_ref = bf16[2,4,4,16,128]{4,3,2,1,0:T(8,128)(2,1)S(1)} all-gather(bf16[1,4,4,16,128]{4,3,2,1,0:T(8,128)(2,1)S(1)} %fusion.1), channel_id=1, replica_groups=mesh['zh'=4,'z1'=2,'z0'=2,'xl'=2,'xh'=2,'y'=4,'core'=2] {'z1'}, dimensions={0}, use_global_device_ids=true | all-gather | bytes 196608 | tf_op jit(solution)/shard_map/all_gather | solution.py:205
  192.0 0.1 deal.5
  192.1 19.9 %all_to_all.44 = bf16[64,3,16,128]{3,2,1,0:T(8,128)(2,1)S(1)} all-to-all(bf16[64,3,16,128]{3,2,1,0:T(8,128)(2,1)S(1)} %bitcast.47), channel_id=1, replica_groups=mesh['zh'=4,'z1'=2,'z0'=2,'xl'=2,'xh'=2,'y'=4,'core'=2] {'z0','xl','xh',..., dimensions={0} | all-to-all | bytes 1572864 | tf_op jit(solution)/shard_map/all_to_all | solution.py:168
  212.0 6.1 %terms.5 = bf16[4,16,3,16,128]{4,3,2,1,0:T(8,128)(2,1)} custom-call(s32[608]{0:T(1024)S(1)} %pad_add_fusion.index, bf16[4,16,3,16,128]{4,3,2,1,0:T(8,128)(2,1)S(1)} %bitcast.50, bf16[152,128,128]{2,1,0:T(8,128)(2,1)} %bitcast.62), custom_call_target="tpu_custom_call" | custom-call | tf_op jit(solution)/shard_map/terms/pallas_call | solution.py:90
  218.1 6.0 %all-to-all-start.6 = ((bf16[64,3,16,128]{3,2,1,0:T(8,128)(2,1)}), bf16[64,3,16,128]{3,2,1,0:T(8,128)(2,1)S(1)}, u32[]{:S(2)}, u32[]{:S(2)}) async-start(bf16[64,3,16,128]{3,2,1,0:T(8,128)(2,1)} %bitcast.21), calls=%async_computation.6 | async-start | bytes 1572864 | tf_op jit(solution)/shard_map/all_to_all | solution.py:168
  224.2 13.7 %all-to-all-done.6 = bf16[64,3,16,128]{3,2,1,0:T(8,128)(2,1)S(1)} async-done(((bf16[64,3,16,128]{3,2,1,0:T(8,128)(2,1)}), bf16[64,3,16,128]{3,2,1,0:T(8,128)(2,1)S(1)}, u32[]{:S(2)}, u32[]{:S(2)}) %all-to-all-start.6) | async-done | bytes 786464 | tf_op jit(solution)/shard_map/all_to_all | solution.py:168
  237.9 0.1 merge.5
  238.0 23.7 %all_to_all.45 = bf16[32,16,128]{2,1,0:T(8,128)(2,1)S(1)} all-to-all(bf16[32,16,128]{2,1,0:T(8,128)(2,1)S(1)} %bitcast.59), channel_id=1, replica_groups=mesh['zh'=4,'z1'=2,'z0'=2,'xl'=2,'xh'=2,'y'=4,'core'=2] {'z1','zh','z0',..., dimensions={0} | all-to-all | bytes 262144 | tf_op jit(solution)/shard_map/all_to_all | solution.py:168
  261.7 0.6 convert_reduce_fusion.2
  (10 shorter events, 0.3 us)
Async XLA Ops:
  32.8 22.6 %all-to-all-start.1 = ((bf16[64,3,16,128]{3,2,1,0:T(8,128)(2,1)}), bf16[64,3,16,128]{3,2,1,0:T(8,128)(2,1)S(1)}, u32[]{:S(2)}, u32[]{:S(2)}) async-start(bf16[64,3,16,128]{3,2,1,0:T(8,128)(2,1)} %bitcast.6), calls=%async_computation.1 | async-start | bytes 1572864 | tf_op jit(solution)/shard_map/all_to_all | solution.py:168
  80.4 7.1 %collective-permute-start = (bf16[4,4,16,128]{3,2,1,0:T(8,128)(2,1)S(1)}, bf16[4,4,16,128]{3,2,1,0:T(8,128)(2,1)S(1)}, u32[]{:S(2)}, u32[]{:S(2)}) collective-permute-start(bf16[4,4,16,128]{3,2,1,0:T(8,128)(2,1)S(1)} %get-tuple-element.10), channel_id=1, source_target_pairs={{0,64},{64,0},{1,65},{65,1},{2,66},{66,2},{3,67},{67,3},{4,68},{68... | collective-permute-start | bytes 196616 | tf_op jit(solution)/shard_map/ppermute | solution.py:199
  158.9 7.1 %collective-permute-start.1 = (bf16[4,4,16,128]{3,2,1,0:T(8,128)(2,1)S(1)}, bf16[4,4,16,128]{3,2,1,0:T(8,128)(2,1)S(1)}, u32[]{:S(2)}, u32[]{:S(2)}) collective-permute-start(bf16[4,4,16,128]{3,2,1,0:T(8,128)(2,1)S(1)} %get-tuple-element.12), channel_id=1, source_target_pairs={{0,64},{64,0},{1,65},{65,1},{2,66},{66,2},{3,67},{67,3},{4,68},{68... | collective-permute-start | bytes 196616 | tf_op jit(solution)/shard_map/ppermute | solution.py:199
  218.1 19.8 %all-to-all-start.6 = ((bf16[64,3,16,128]{3,2,1,0:T(8,128)(2,1)}), bf16[64,3,16,128]{3,2,1,0:T(8,128)(2,1)S(1)}, u32[]{:S(2)}, u32[]{:S(2)}) async-start(bf16[64,3,16,128]{3,2,1,0:T(8,128)(2,1)} %bitcast.21), calls=%async_computation.6 | async-start | bytes 1572864 | tf_op jit(solution)/shard_map/all_to_all | solution.py:168

commit v6 on v5

--- a/solution.py
+++ b/solution.py
@@ -197,7 +197,8 @@
     for step in range(DEGREE - 1):
         kept, sent = unit_sums(wire)
         pair_sums = kept + lax.ppermute(sent, "z1", [(0, 1), (1, 0)]).astype(FLOAT)
-        image = total(lax.all_gather(pair_sums.astype(WIRE), "zh"))
+        far = total(lax.all_gather(pair_sums[1:].astype(WIRE), "zh"))
+        image = jnp.concatenate([pair_sums[:1], far])
         after = (image - CENTER * now) / HALF_WIDTH
         if step > 0:
             after = 2.0 * (image - CENTER * now) / HALF_WIDTH - before

time: 263 us -> 261 us (level)
  the two profiles are of different devices: /device:TPU:32 before, /device:TPU:4 now
where the time goes in v6:
time: 261 us; the launch traced here: 260 us
  blocking collectives  183 us (70%)
  waiting for transfers between devices  32.6 us (12%)
  starting transfers between devices  21.5 us (8%)
  Pallas kernels  18.2 us (7%)
  other arithmetic  3.8 us (1%)
    all_to_all x6, blocking collectives, exchange(): return lax.all_to_all(x, axes, 0, 0, tiled=True)  133 us
    all_gather x2, blocking collectives, local(): far = total(lax.all_gather(pair_sums[1:].astype(WIRE), 'zh'))  38.2 us
    all_to_all x2, waiting for transfers between devices, exchange(): return lax.all_to_all(x, axes, 0, 0, tiled=True)  22.5 us
    pallas_call x3, Pallas kernels, terms(): pl.pallas_call(terms_kernel, out_shape=jax.ShapeDtypeStruct(x.shape, WIRE...  16.7 us
    all_to_all x2, starting transfers between devices, exchange(): return lax.all_to_all(x, axes, 0, 0, tiled=True)  15 us
    all_gather x2, blocking collectives, local(): wire = lax.all_gather(now.astype(WIRE), 'z1')  11.7 us
    ppermute x2, waiting for transfers between devices, local(): pair_sums = kept + lax.ppermute(sent, 'z1', [(0, 1), (1, 0)]).astype(FLOAT)  10.1 us
    ppermute x2, starting transfers between devices, local(): pair_sums = kept + lax.ppermute(sent, 'z1', [(0, 1), (1, 0)]).astype(FLOAT)  6.46 us
  transfers between devices with their start and end apart: 4, of which 4 were waited for; matrix products, arithmetic and copies ran while one was open for 1% of the time, Pallas kernels for 0%

profile of v6, /device:TPU:4, one launch (start us, length us, event | category | flops | bytes accessed | tf_op | source)
XLA Modules:
  0.0 260.2 jit_solution(8981033683195035935)
XLA Ops:
  0.0 0.8 convert_element_type.41
  0.8 32.1 %all_to_all.40 = bf16[32,16,128]{2,1,0:T(8,128)(2,1)S(1)} all-to-all(bf16[32,16,128]{2,1,0:T(8,128)(2,1)S(1)} %bitcast.65), channel_id=1, replica_groups=mesh['zh'=4,'z1'=2,'z0'=2,'xl'=2,'xh'=2,'y'=4,'core'=2] {'z1','zh','z0',..., dimensions={0} | all-to-all | bytes 262144 | tf_op jit(solution)/shard_map/all_to_all | solution.py:168
  32.9 1.0 deal.3
  33.9 8.0 %all-to-all-start.1 = ((bf16[64,3,16,128]{3,2,1,0:T(8,128)(2,1)}), bf16[64,3,16,128]{3,2,1,0:T(8,128)(2,1)S(1)}, u32[]{:S(2)}, u32[]{:S(2)}) async-start(bf16[64,3,16,128]{3,2,1,0:T(8,128)(2,1)} %bitcast.6), calls=%async_computation.1 | async-start | bytes 1572864 | tf_op jit(solution)/shard_map/all_to_all | solution.py:168
  42.6 0.7 broadcast_select_fusion.1
  43.3 0.7 broadcast_select_fusion
  44.0 0.8 pad_add_fusion.index
  44.8 9.9 %all-to-all-done.1 = bf16[64,3,16,128]{3,2,1,0:T(8,128)(2,1)S(1)} async-done(((bf16[64,3,16,128]{3,2,1,0:T(8,128)(2,1)}), bf16[64,3,16,128]{3,2,1,0:T(8,128)(2,1)S(1)}, u32[]{:S(2)}, u32[]{:S(2)}) %all-to-all-start.1) | async-done | bytes 786464 | tf_op jit(solution)/shard_map/all_to_all | solution.py:168
  54.7 5.3 %terms.3 = bf16[4,16,3,16,128]{4,3,2,1,0:T(8,128)(2,1)S(1)} custom-call(s32[608]{0:T(1024)S(1)} %pad_add_fusion.index, bf16[4,16,3,16,128]{4,3,2,1,0:T(8,128)(2,1)S(1)} %bitcast.45, bf16[152,128,128]{2,1,0:T(8,128)(2,1)} %bitcast.56), custom_call_target="tpu_custom_call" | custom-call | tf_op jit(solution)/shard_map/terms/pallas_call | solution.py:90
  59.9 19.5 %all_to_all.41 = bf16[64,3,16,128]{3,2,1,0:T(8,128)(2,1)S(1)} all-to-all(bf16[64,3,16,128]{3,2,1,0:T(8,128)(2,1)S(1)} %bitcast.47), channel_id=1, replica_groups=mesh['zh'=4,'z1'=2,'z0'=2,'xl'=2,'xh'=2,'y'=4,'core'=2] {'z0','xl','xh',..., dimensions={0} | all-to-all | bytes 1572864 | tf_op jit(solution)/shard_map/all_to_all | solution.py:168
  79.5 0.1 merge.3
  79.6 3.0 %collective-permute-start = (bf16[4,4,16,128]{3,2,1,0:T(8,128)(2,1)S(1)}, bf16[4,4,16,128]{3,2,1,0:T(8,128)(2,1)S(1)}, u32[]{:S(2)}, u32[]{:S(2)}) collective-permute-start(bf16[4,4,16,128]{3,2,1,0:T(8,128)(2,1)S(1)} %get-tuple-element.10), channel_id=1, source_target_pairs={{0,64},{64,0},{1,65},{65,1},{2,66},{66,2},{3,67},{67,3},{4,68},{68... | collective-permute-start | bytes 196616 | tf_op jit(solution)/shard_map/ppermute | solution.py:199
  82.6 5.3 %collective-permute-done = bf16[4,4,16,128]{3,2,1,0:T(8,128)(2,1)S(1)} collective-permute-done((bf16[4,4,16,128]{3,2,1,0:T(8,128)(2,1)S(1)}, bf16[4,4,16,128]{3,2,1,0:T(8,128)(2,1)S(1)}, u32[]{:S(2)}, u32[]{:S(2)}) %collective-permute-start) | collective-permute-done | bytes 65568 | tf_op jit(solution)/shard_map/ppermute | solution.py:199
  87.9 19.2 %all-gather = bf16[12,4,16,128]{3,2,1,0:T(8,128)(2,1)S(1)} all-gather(bf16[3,4,16,128]{3,2,1,0:T(8,128)(2,1)S(1)} %slice.27), channel_id=2, replica_groups=mesh['zh'=4,'z1'=2,'z0'=2,'xl'=2,'xh'=2,'y'=4,'core'=2] {'zh'}, dimensions={0}, use_global_device_ids=true | all-gather | bytes 245760 | tf_op jit(solution)/shard_map/all_gather | solution.py:200
  107.2 5.8 %all_gather.22.all_ref = bf16[2,4,4,16,128]{4,3,2,1,0:T(8,128)(2,1)S(1)} all-gather(bf16[1,4,4,16,128]{4,3,2,1,0:T(8,128)(2,1)S(1)} %multiply_convert_fusion), channel_id=1, replica_groups=mesh['zh'=4,'z1'=2,'z0'=2,'xl'=2,'xh'=2,'y'=4,'core'=2] {'z1'}, dimensions={0}, use_global_device_ids=true | all-gather | bytes 196608 | tf_op jit(solution)/shard_map/all_gather | solution.py:206
  113.0 0.1 deal.4
  113.1 18.5 %all_to_all.42 = bf16[64,3,16,128]{3,2,1,0:T(8,128)(2,1)S(1)} all-to-all(bf16[64,3,16,128]{3,2,1,0:T(8,128)(2,1)S(1)} %bitcast.42), channel_id=1, replica_groups=mesh['zh'=4,'z1'=2,'z0'=2,'xl'=2,'xh'=2,'y'=4,'core'=2] {'z0','xl','xh',..., dimensions={0} | all-to-all | bytes 1572864 | tf_op jit(solution)/shard_map/all_to_all | solution.py:168
  131.6 5.3 %terms.4 = bf16[4,16,3,16,128]{4,3,2,1,0:T(8,128)(2,1)S(1)} custom-call(s32[608]{0:T(1024)S(1)} %pad_add_fusion.index, bf16[4,16,3,16,128]{4,3,2,1,0:T(8,128)(2,1)S(1)} %bitcast.48, bf16[152,128,128]{2,1,0:T(8,128)(2,1)} %bitcast.57), custom_call_target="tpu_custom_call" | custom-call | tf_op jit(solution)/shard_map/terms/pallas_call | solution.py:90
  136.9 19.5 %all_to_all.43 = bf16[64,3,16,128]{3,2,1,0:T(8,128)(2,1)S(1)} all-to-all(bf16[64,3,16,128]{3,2,1,0:T(8,128)(2,1)S(1)} %bitcast.49), channel_id=1, replica_groups=mesh['zh'=4,'z1'=2,'z0'=2,'xl'=2,'xh'=2,'y'=4,'core'=2] {'z0','xl','xh',..., dimensions={0} | all-to-all | bytes 1572864 | tf_op jit(solution)/shard_map/all_to_all | solution.py:168
  156.4 0.1 merge.4
  156.5 3.5 %collective-permute-start.1 = (bf16[4,4,16,128]{3,2,1,0:T(8,128)(2,1)S(1)}, bf16[4,4,16,128]{3,2,1,0:T(8,128)(2,1)S(1)}, u32[]{:S(2)}, u32[]{:S(2)}) collective-permute-start(bf16[4,4,16,128]{3,2,1,0:T(8,128)(2,1)S(1)} %get-tuple-element.12), channel_id=1, source_target_pairs={{0,64},{64,0},{1,65},{65,1},{2,66},{66,2},{3,67},{67,3},{4,68},{68... | collective-permute-start | bytes 196616 | tf_op jit(solution)/shard_map/ppermute | solution.py:199
  160.0 4.8 %collective-permute-done.1 = bf16[4,4,16,128]{3,2,1,0:T(8,128)(2,1)S(1)} collective-permute-done((bf16[4,4,16,128]{3,2,1,0:T(8,128)(2,1)S(1)}, bf16[4,4,16,128]{3,2,1,0:T(8,128)(2,1)S(1)}, u32[]{:S(2)}, u32[]{:S(2)}) %collective-permute-start.1) | collective-permute-done | bytes 65568 | tf_op jit(solution)/shard_map/ppermute | solution.py:199
  164.8 19.0 %all-gather.1 = bf16[12,4,16,128]{3,2,1,0:T(8,128)(2,1)S(1)} all-gather(bf16[3,4,16,128]{3,2,1,0:T(8,128)(2,1)S(1)} %slice.26), channel_id=3, replica_groups=mesh['zh'=4,'z1'=2,'z0'=2,'xl'=2,'xh'=2,'y'=4,'core'=2] {'zh'}, dimensions={0}, use_global_device_ids=true | all-gather | bytes 245760 | tf_op jit(solution)/shard_map/all_gather | solution.py:200
  183.9 5.9 %all_gather.25.all_ref = bf16[2,4,4,16,128]{4,3,2,1,0:T(8,128)(2,1)S(1)} all-gather(bf16[1,4,4,16,128]{4,3,2,1,0:T(8,128)(2,1)S(1)} %fusion.1), channel_id=1, replica_groups=mesh['zh'=4,'z1'=2,'z0'=2,'xl'=2,'xh'=2,'y'=4,'core'=2] {'z1'}, dimensions={0}, use_global_device_ids=true | all-gather | bytes 196608 | tf_op jit(solution)/shard_map/all_gather | solution.py:206
  189.8 0.1 deal.5
  189.9 18.6 %all_to_all.44 = bf16[64,3,16,128]{3,2,1,0:T(8,128)(2,1)S(1)} all-to-all(bf16[64,3,16,128]{3,2,1,0:T(8,128)(2,1)S(1)} %bitcast.43), channel_id=1, replica_groups=mesh['zh'=4,'z1'=2,'z0'=2,'xl'=2,'xh'=2,'y'=4,'core'=2] {'z0','xl','xh',..., dimensions={0} | all-to-all | bytes 1572864 | tf_op jit(solution)/shard_map/all_to_all | solution.py:168
  208.5 6.2 %terms.5 = bf16[4,16,3,16,128]{4,3,2,1,0:T(8,128)(2,1)} custom-call(s32[608]{0:T(1024)S(1)} %pad_add_fusion.index, bf16[4,16,3,16,128]{4,3,2,1,0:T(8,128)(2,1)S(1)} %bitcast.46, bf16[152,128,128]{2,1,0:T(8,128)(2,1)} %bitcast.58), custom_call_target="tpu_custom_call" | custom-call | tf_op jit(solution)/shard_map/terms/pallas_call | solution.py:90
  214.7 7.0 %all-to-all-start.6 = ((bf16[64,3,16,128]{3,2,1,0:T(8,128)(2,1)}), bf16[64,3,16,128]{3,2,1,0:T(8,128)(2,1)S(1)}, u32[]{:S(2)}, u32[]{:S(2)}) async-start(bf16[64,3,16,128]{3,2,1,0:T(8,128)(2,1)} %bitcast.23), calls=%async_computation.6 | async-start | bytes 1572864 | tf_op jit(solution)/shard_map/all_to_all | solution.py:168
  221.8 12.6 %all-to-all-done.6 = bf16[64,3,16,128]{3,2,1,0:T(8,128)(2,1)S(1)} async-done(((bf16[64,3,16,128]{3,2,1,0:T(8,128)(2,1)}), bf16[64,3,16,128]{3,2,1,0:T(8,128)(2,1)S(1)}, u32[]{:S(2)}, u32[]{:S(2)}) %all-to-all-start.6) | async-done | bytes 786464 | tf_op jit(solution)/shard_map/all_to_all | solution.py:168
  234.4 0.1 merge.5
  234.5 25.0 %all_to_all.45 = bf16[32,16,128]{2,1,0:T(8,128)(2,1)S(1)} all-to-all(bf16[32,16,128]{2,1,0:T(8,128)(2,1)S(1)} %bitcast.55), channel_id=1, replica_groups=mesh['zh'=4,'z1'=2,'z0'=2,'xl'=2,'xh'=2,'y'=4,'core'=2] {'z1','zh','z0',..., dimensions={0} | all-to-all | bytes 262144 | tf_op jit(solution)/shard_map/all_to_all | solution.py:168
  259.6 0.6 convert_reduce_fusion.2
  (14 shorter events, 0.3 us)
Async XLA Ops:
  33.9 20.7 %all-to-all-start.1 = ((bf16[64,3,16,128]{3,2,1,0:T(8,128)(2,1)}), bf16[64,3,16,128]{3,2,1,0:T(8,128)(2,1)S(1)}, u32[]{:S(2)}, u32[]{:S(2)}) async-start(bf16[64,3,16,128]{3,2,1,0:T(8,128)(2,1)} %bitcast.6), calls=%async_computation.1 | async-start | bytes 1572864 | tf_op jit(solution)/shard_map/all_to_all | solution.py:168
  79.6 8.3 %collective-permute-start = (bf16[4,4,16,128]{3,2,1,0:T(8,128)(2,1)S(1)}, bf16[4,4,16,128]{3,2,1,0:T(8,128)(2,1)S(1)}, u32[]{:S(2)}, u32[]{:S(2)}) collective-permute-start(bf16[4,4,16,128]{3,2,1,0:T(8,128)(2,1)S(1)} %get-tuple-element.10), channel_id=1, source_target_pairs={{0,64},{64,0},{1,65},{65,1},{2,66},{66,2},{3,67},{67,3},{4,68},{68... | collective-permute-start | bytes 196616 | tf_op jit(solution)/shard_map/ppermute | solution.py:199
  156.5 8.3 %collective-permute-start.1 = (bf16[4,4,16,128]{3,2,1,0:T(8,128)(2,1)S(1)}, bf16[4,4,16,128]{3,2,1,0:T(8,128)(2,1)S(1)}, u32[]{:S(2)}, u32[]{:S(2)}) collective-permute-start(bf16[4,4,16,128]{3,2,1,0:T(8,128)(2,1)S(1)} %get-tuple-element.12), channel_id=1, source_target_pairs={{0,64},{64,0},{1,65},{65,1},{2,66},{66,2},{3,67},{67,3},{4,68},{68... | collective-permute-start | bytes 196616 | tf_op jit(solution)/shard_map/ppermute | solution.py:199
  214.7 19.8 %all-to-all-start.6 = ((bf16[64,3,16,128]{3,2,1,0:T(8,128)(2,1)}), bf16[64,3,16,128]{3,2,1,0:T(8,128)(2,1)S(1)}, u32[]{:S(2)}, u32[]{:S(2)}) async-start(bf16[64,3,16,128]{3,2,1,0:T(8,128)(2,1)} %bitcast.23), calls=%async_computation.6 | async-start | bytes 1572864 | tf_op jit(solution)/shard_map/all_to_all | solution.py:168

commit v7 on v6

--- a/solution.py
+++ b/solution.py
@@ -10,7 +10,7 @@
 CENTER = 0.25
 HALF_WIDTH = 2.0
 DEGREE = 3
-CHUNKS, AHEAD = 4, 2
+FIRST, CHUNKS, AHEAD = 8, 5, 2
 QUAD = ("z0", "xl")
 ROW = ("zh", "z1") + QUAD
 COL = ("xh", "y", "core")
@@ -39,28 +39,16 @@
 
 def terms_kernel(index, x_ref, blocks_hbm, out_ref, col_acc, row_acc, blocks, sems):
     slots, size = blocks.shape[:2]
-    part = slots // CHUNKS
+    part = (slots - FIRST) // (CHUNKS - 1)
     width = x_ref.shape[0] * x_ref.shape[3]
     share = x_ref.shape[3]
 
     def copy(i):
-        here = pl.ds(i * part, part)
+        here = pl.ds(0, FIRST) if isinstance(i, int) and i == 0 else pl.ds(FIRST + (i - 1) * part, part)
         return pltpu.make_async_copy(blocks_hbm.at[here], blocks.at[here], sems.at[i])
 
-    for i in range(AHEAD):
-        copy(i).start()
-    col_acc[...] = jnp.zeros_like(col_acc)
-    row_acc[...] = jnp.zeros_like(row_acc)
-
-    def chunk(i, carry):
-        base = i * part
-        copy(i).wait()
-
-        @pl.when(i + AHEAD < CHUNKS)
-        def _():
-            copy(i + AHEAD).start()
-
-        for s in range(0, part, 2):
+    def work(base, count):
+        for s in range(0, count, 2):
             pair = (base + s, base + s + 1)
             both = [blocks[t] for t in pair]
             x_row = [x_ref[:, index[t], N_HALF].reshape(width, size) for t in pair]
@@ -74,9 +62,25 @@
                 col_acc[to] = col_acc[to] + by_col[own]
                 to = index[2 * slots + t]
                 row_acc[to] = row_acc[to] + by_row[own]
+
+    for i in range(AHEAD + 1):
+        copy(i).start()
+    col_acc[...] = jnp.zeros_like(col_acc)
+    row_acc[...] = jnp.zeros_like(row_acc)
+    copy(0).wait()
+    work(0, FIRST)
+
+    def chunk(i, carry):
+        copy(i).wait()
+
+        @pl.when(i + AHEAD < CHUNKS)
+        def _():
+            copy(i + AHEAD).start()
+
+        work(FIRST + (i - 1) * part, part)
         return carry
 
-    lax.fori_loop(0, CHUNKS, chunk, 0)
+    lax.fori_loop(1, CHUNKS, chunk, 0)
     for k in range(x_ref.shape[0]):
         lines = slice(k * share, (k + 1) * share)
         for h in range(N_HALF):

time: 261 us -> 261 us (level)
  no operation moved by 1% of the time
where the time goes in v7:
time: 261 us; the launch traced here: 260 us
  blocking collectives  183 us (70%)
  waiting for transfers between devices  33 us (13%)
  starting transfers between devices  21.1 us (8%)
  Pallas kernels  18.1 us (7%)
  other arithmetic  3.8 us (1%)
    all_to_all x6, blocking collectives, exchange(): return lax.all_to_all(x, axes, 0, 0, tiled=True)  134 us
    all_gather x2, blocking collectives, local(): far = total(lax.all_gather(pair_sums[1:].astype(WIRE), 'zh'))  37 us
    all_to_all x2, waiting for transfers between devices, exchange(): return lax.all_to_all(x, axes, 0, 0, tiled=True)  22.5 us
    pallas_call x3, Pallas kernels, terms(): pl.pallas_call(terms_kernel, out_shape=jax.ShapeDtypeStruct(x.shape, WIRE...  16.5 us
    all_to_all x2, starting transfers between devices, exchange(): return lax.all_to_all(x, axes, 0, 0, tiled=True)  15 us
    all_gather x2, blocking collectives, local(): wire = lax.all_gather(now.astype(WIRE), 'z1')  12.4 us
    ppermute x2, waiting for transfers between devices, local(): pair_sums = kept + lax.ppermute(sent, 'z1', [(0, 1), (1, 0)]).astype(FLOAT)  10.5 us
    ppermute x2, starting transfers between devices, local(): pair_sums = kept + lax.ppermute(sent, 'z1', [(0, 1), (1, 0)]).astype(FLOAT)  6.07 us
  transfers between devices with their start and end apart: 4, of which 4 were waited for; matrix products, arithmetic and copies ran while one was open for 1% of the time, Pallas kernels for 0%

profile of v7, /device:TPU:4, one launch (start us, length us, event | category | flops | bytes accessed | tf_op | source)
XLA Modules:
  0.0 260.1 jit_solution(7227355113791865704)
XLA Ops:
  0.0 0.8 convert_element_type.41
  0.8 32.1 %all_to_all.40 = bf16[32,16,128]{2,1,0:T(8,128)(2,1)S(1)} all-to-all(bf16[32,16,128]{2,1,0:T(8,128)(2,1)S(1)} %bitcast.65), channel_id=1, replica_groups=mesh['zh'=4,'z1'=2,'z0'=2,'xl'=2,'xh'=2,'y'=4,'core'=2] {'z1','zh','z0',..., dimensions={0} | all-to-all | bytes 262144 | tf_op jit(solution)/shard_map/all_to_all | solution.py:172
  32.9 1.0 deal.3
  33.9 8.0 %all-to-all-start.1 = ((bf16[64,3,16,128]{3,2,1,0:T(8,128)(2,1)}), bf16[64,3,16,128]{3,2,1,0:T(8,128)(2,1)S(1)}, u32[]{:S(2)}, u32[]{:S(2)}) async-start(bf16[64,3,16,128]{3,2,1,0:T(8,128)(2,1)} %bitcast.6), calls=%async_computation.1 | async-start | bytes 1572864 | tf_op jit(solution)/shard_map/all_to_all | solution.py:172
  42.6 0.7 broadcast_select_fusion.1
  43.3 0.7 broadcast_select_fusion
  44.0 0.8 pad_add_fusion.index
  44.8 9.9 %all-to-all-done.1 = bf16[64,3,16,128]{3,2,1,0:T(8,128)(2,1)S(1)} async-done(((bf16[64,3,16,128]{3,2,1,0:T(8,128)(2,1)}), bf16[64,3,16,128]{3,2,1,0:T(8,128)(2,1)S(1)}, u32[]{:S(2)}, u32[]{:S(2)}) %all-to-all-start.1) | async-done | bytes 786464 | tf_op jit(solution)/shard_map/all_to_all | solution.py:172
  54.7 5.2 %terms.3 = bf16[4,16,3,16,128]{4,3,2,1,0:T(8,128)(2,1)S(1)} custom-call(s32[608]{0:T(1024)S(1)} %pad_add_fusion.index, bf16[4,16,3,16,128]{4,3,2,1,0:T(8,128)(2,1)S(1)} %bitcast.45, bf16[152,128,128]{2,1,0:T(8,128)(2,1)} %bitcast.56), custom_call_target="tpu_custom_call" | custom-call | tf_op jit(solution)/shard_map/terms/pallas_call | solution.py:94
  59.9 19.5 %all_to_all.41 = bf16[64,3,16,128]{3,2,1,0:T(8,128)(2,1)S(1)} all-to-all(bf16[64,3,16,128]{3,2,1,0:T(8,128)(2,1)S(1)} %bitcast.47), channel_id=1, replica_groups=mesh['zh'=4,'z1'=2,'z0'=2,'xl'=2,'xh'=2,'y'=4,'core'=2] {'z0','xl','xh',..., dimensions={0} | all-to-all | bytes 1572864 | tf_op jit(solution)/shard_map/all_to_all | solution.py:172
  79.4 0.1 merge.3
  79.5 3.0 %collective-permute-start = (bf16[4,4,16,128]{3,2,1,0:T(8,128)(2,1)S(1)}, bf16[4,4,16,128]{3,2,1,0:T(8,128)(2,1)S(1)}, u32[]{:S(2)}, u32[]{:S(2)}) collective-permute-start(bf16[4,4,16,128]{3,2,1,0:T(8,128)(2,1)S(1)} %get-tuple-element.10), channel_id=1, source_target_pairs={{0,64},{64,0},{1,65},{65,1},{2,66},{66,2},{3,67},{67,3},{4,68},{68... | collective-permute-start | bytes 196616 | tf_op jit(solution)/shard_map/ppermute | solution.py:203
  82.5 5.3 %collective-permute-done = bf16[4,4,16,128]{3,2,1,0:T(8,128)(2,1)S(1)} collective-permute-done((bf16[4,4,16,128]{3,2,1,0:T(8,128)(2,1)S(1)}, bf16[4,4,16,128]{3,2,1,0:T(8,128)(2,1)S(1)}, u32[]{:S(2)}, u32[]{:S(2)}) %collective-permute-start) | collective-permute-done | bytes 65568 | tf_op jit(solution)/shard_map/ppermute | solution.py:203
  87.8 19.2 %all-gather = bf16[12,4,16,128]{3,2,1,0:T(8,128)(2,1)S(1)} all-gather(bf16[3,4,16,128]{3,2,1,0:T(8,128)(2,1)S(1)} %slice.27), channel_id=2, replica_groups=mesh['zh'=4,'z1'=2,'z0'=2,'xl'=2,'xh'=2,'y'=4,'core'=2] {'zh'}, dimensions={0}, use_global_device_ids=true | all-gather | bytes 245760 | tf_op jit(solution)/shard_map/all_gather | solution.py:204
  107.1 5.8 %all_gather.22.all_ref = bf16[2,4,4,16,128]{4,3,2,1,0:T(8,128)(2,1)S(1)} all-gather(bf16[1,4,4,16,128]{4,3,2,1,0:T(8,128)(2,1)S(1)} %multiply_convert_fusion), channel_id=1, replica_groups=mesh['zh'=4,'z1'=2,'z0'=2,'xl'=2,'xh'=2,'y'=4,'core'=2] {'z1'}, dimensions={0}, use_global_device_ids=true | all-gather | bytes 196608 | tf_op jit(solution)/shard_map/all_gather | solution.py:210
  112.9 0.1 deal.4
  113.0 18.8 %all_to_all.42 = bf16[64,3,16,128]{3,2,1,0:T(8,128)(2,1)S(1)} all-to-all(bf16[64,3,16,128]{3,2,1,0:T(8,128)(2,1)S(1)} %bitcast.42), channel_id=1, replica_groups=mesh['zh'=4,'z1'=2,'z0'=2,'xl'=2,'xh'=2,'y'=4,'core'=2] {'z0','xl','xh',..., dimensions={0} | all-to-all | bytes 1572864 | tf_op jit(solution)/shard_map/all_to_all | solution.py:172
  131.8 5.2 %terms.4 = bf16[4,16,3,16,128]{4,3,2,1,0:T(8,128)(2,1)S(1)} custom-call(s32[608]{0:T(1024)S(1)} %pad_add_fusion.index, bf16[4,16,3,16,128]{4,3,2,1,0:T(8,128)(2,1)S(1)} %bitcast.48, bf16[152,128,128]{2,1,0:T(8,128)(2,1)} %bitcast.57), custom_call_target="tpu_custom_call" | custom-call | tf_op jit(solution)/shard_map/terms/pallas_call | solution.py:94
  137.0 19.5 %all_to_all.43 = bf16[64,3,16,128]{3,2,1,0:T(8,128)(2,1)S(1)} all-to-all(bf16[64,3,16,128]{3,2,1,0:T(8,128)(2,1)S(1)} %bitcast.49), channel_id=1, replica_groups=mesh['zh'=4,'z1'=2,'z0'=2,'xl'=2,'xh'=2,'y'=4,'core'=2] {'z0','xl','xh',..., dimensions={0} | all-to-all | bytes 1572864 | tf_op jit(solution)/shard_map/all_to_all | solution.py:172
  156.5 0.1 merge.4
  156.7 3.1 %collective-permute-start.1 = (bf16[4,4,16,128]{3,2,1,0:T(8,128)(2,1)S(1)}, bf16[4,4,16,128]{3,2,1,0:T(8,128)(2,1)S(1)}, u32[]{:S(2)}, u32[]{:S(2)}) collective-permute-start(bf16[4,4,16,128]{3,2,1,0:T(8,128)(2,1)S(1)} %get-tuple-element.12), channel_id=1, source_target_pairs={{0,64},{64,0},{1,65},{65,1},{2,66},{66,2},{3,67},{67,3},{4,68},{68... | collective-permute-start | bytes 196616 | tf_op jit(solution)/shard_map/ppermute | solution.py:203
  159.8 5.2 %collective-permute-done.1 = bf16[4,4,16,128]{3,2,1,0:T(8,128)(2,1)S(1)} collective-permute-done((bf16[4,4,16,128]{3,2,1,0:T(8,128)(2,1)S(1)}, bf16[4,4,16,128]{3,2,1,0:T(8,128)(2,1)S(1)}, u32[]{:S(2)}, u32[]{:S(2)}) %collective-permute-start.1) | collective-permute-done | bytes 65568 | tf_op jit(solution)/shard_map/ppermute | solution.py:203
  165.0 17.8 %all-gather.1 = bf16[12,4,16,128]{3,2,1,0:T(8,128)(2,1)S(1)} all-gather(bf16[3,4,16,128]{3,2,1,0:T(8,128)(2,1)S(1)} %slice.26), channel_id=3, replica_groups=mesh['zh'=4,'z1'=2,'z0'=2,'xl'=2,'xh'=2,'y'=4,'core'=2] {'zh'}, dimensions={0}, use_global_device_ids=true | all-gather | bytes 245760 | tf_op jit(solution)/shard_map/all_gather | solution.py:204
  182.9 6.5 %all_gather.25.all_ref = bf16[2,4,4,16,128]{4,3,2,1,0:T(8,128)(2,1)S(1)} all-gather(bf16[1,4,4,16,128]{4,3,2,1,0:T(8,128)(2,1)S(1)} %fusion.1), channel_id=1, replica_groups=mesh['zh'=4,'z1'=2,'z0'=2,'xl'=2,'xh'=2,'y'=4,'core'=2] {'z1'}, dimensions={0}, use_global_device_ids=true | all-gather | bytes 196608 | tf_op jit(solution)/shard_map/all_gather | solution.py:210
  189.5 0.1 deal.5
  189.6 19.1 %all_to_all.44 = bf16[64,3,16,128]{3,2,1,0:T(8,128)(2,1)S(1)} all-to-all(bf16[64,3,16,128]{3,2,1,0:T(8,128)(2,1)S(1)} %bitcast.43), channel_id=1, replica_groups=mesh['zh'=4,'z1'=2,'z0'=2,'xl'=2,'xh'=2,'y'=4,'core'=2] {'z0','xl','xh',..., dimensions={0} | all-to-all | bytes 1572864 | tf_op jit(solution)/shard_map/all_to_all | solution.py:172
  208.6 6.1 %terms.5 = bf16[4,16,3,16,128]{4,3,2,1,0:T(8,128)(2,1)} custom-call(s32[608]{0:T(1024)S(1)} %pad_add_fusion.index, bf16[4,16,3,16,128]{4,3,2,1,0:T(8,128)(2,1)S(1)} %bitcast.46, bf16[152,128,128]{2,1,0:T(8,128)(2,1)} %bitcast.58), custom_call_target="tpu_custom_call" | custom-call | tf_op jit(solution)/shard_map/terms/pallas_call | solution.py:94
  214.7 7.0 %all-to-all-start.6 = ((bf16[64,3,16,128]{3,2,1,0:T(8,128)(2,1)}), bf16[64,3,16,128]{3,2,1,0:T(8,128)(2,1)S(1)}, u32[]{:S(2)}, u32[]{:S(2)}) async-start(bf16[64,3,16,128]{3,2,1,0:T(8,128)(2,1)} %bitcast.23), calls=%async_computation.6 | async-start | bytes 1572864 | tf_op jit(solution)/shard_map/all_to_all | solution.py:172
  221.9 12.6 %all-to-all-done.6 = bf16[64,3,16,128]{3,2,1,0:T(8,128)(2,1)S(1)} async-done(((bf16[64,3,16,128]{3,2,1,0:T(8,128)(2,1)}), bf16[64,3,16,128]{3,2,1,0:T(8,128)(2,1)S(1)}, u32[]{:S(2)}, u32[]{:S(2)}) %all-to-all-start.6) | async-done | bytes 786464 | tf_op jit(solution)/shard_map/all_to_all | solution.py:172
  234.5 0.1 merge.5
  234.6 24.8 %all_to_all.45 = bf16[32,16,128]{2,1,0:T(8,128)(2,1)S(1)} all-to-all(bf16[32,16,128]{2,1,0:T(8,128)(2,1)S(1)} %bitcast.55), channel_id=1, replica_groups=mesh['zh'=4,'z1'=2,'z0'=2,'xl'=2,'xh'=2,'y'=4,'core'=2] {'z1','zh','z0',..., dimensions={0} | all-to-all | bytes 262144 | tf_op jit(solution)/shard_map/all_to_all | solution.py:172
  259.4 0.6 convert_reduce_fusion.2
  (14 shorter events, 0.3 us)
Async XLA Ops:
  33.9 20.7 %all-to-all-start.1 = ((bf16[64,3,16,128]{3,2,1,0:T(8,128)(2,1)}), bf16[64,3,16,128]{3,2,1,0:T(8,128)(2,1)S(1)}, u32[]{:S(2)}, u32[]{:S(2)}) async-start(bf16[64,3,16,128]{3,2,1,0:T(8,128)(2,1)} %bitcast.6), calls=%async_computation.1 | async-start | bytes 1572864 | tf_op jit(solution)/shard_map/all_to_all | solution.py:172
  79.5 8.3 %collective-permute-start = (bf16[4,4,16,128]{3,2,1,0:T(8,128)(2,1)S(1)}, bf16[4,4,16,128]{3,2,1,0:T(8,128)(2,1)S(1)}, u32[]{:S(2)}, u32[]{:S(2)}) collective-permute-start(bf16[4,4,16,128]{3,2,1,0:T(8,128)(2,1)S(1)} %get-tuple-element.10), channel_id=1, source_target_pairs={{0,64},{64,0},{1,65},{65,1},{2,66},{66,2},{3,67},{67,3},{4,68},{68... | collective-permute-start | bytes 196616 | tf_op jit(solution)/shard_map/ppermute | solution.py:203
  156.7 8.3 %collective-permute-start.1 = (bf16[4,4,16,128]{3,2,1,0:T(8,128)(2,1)S(1)}, bf16[4,4,16,128]{3,2,1,0:T(8,128)(2,1)S(1)}, u32[]{:S(2)}, u32[]{:S(2)}) collective-permute-start(bf16[4,4,16,128]{3,2,1,0:T(8,128)(2,1)S(1)} %get-tuple-element.12), channel_id=1, source_target_pairs={{0,64},{64,0},{1,65},{65,1},{2,66},{66,2},{3,67},{67,3},{4,68},{68... | collective-permute-start | bytes 196616 | tf_op jit(solution)/shard_map/ppermute | solution.py:203
  214.7 19.8 %all-to-all-start.6 = ((bf16[64,3,16,128]{3,2,1,0:T(8,128)(2,1)}), bf16[64,3,16,128]{3,2,1,0:T(8,128)(2,1)S(1)}, u32[]{:S(2)}, u32[]{:S(2)}) async-start(bf16[64,3,16,128]{3,2,1,0:T(8,128)(2,1)} %bitcast.23), calls=%async_computation.6 | async-start | bytes 1572864 | tf_op jit(solution)/shard_map/all_to_all | solution.py:172
